TPU v7x, 128 devices: a whole 4x4x4 slice. The times are simulated.
128 devices in a mesh: gx: 2 (over core), gy: 64 (over z, y, x).
Axes of the slice: x: 4, y: 4, z: 4, core: 2. Of those that a mesh axis runs over, the one named last changes fastest.
Arguments:
- leaf_multipoles: bfloat16 [524288, 256], P(('gx', 'gy')), may hold values from -6 to 6
- m2m_ops: bfloat16 [8, 256, 256], replicated, may hold values from -0.125 to 0.125
- m2l_ops: bfloat16 [96, 256, 256], replicated, may hold values from -0.0546875 to 0.0546875
- l2l_ops: bfloat16 [8, 256, 256], replicated, may hold values from -0.375 to 0.375
- send_boxes: int32 [128, 3, 64, 128], P(('gx', 'gy')), may hold values from 0 to 511, as said below
- task_source: int32 [128, 96, 512], P(('gx', 'gy')), may hold values from 0 to 25087, as said below
- task_target: int32 [128, 96, 512], P(('gx', 'gy')), may hold values from 0 to 511, as said below
- task_count: int32 [128, 96], P(('gx', 'gy')), may hold values from 1 to 511, as said below
Outputs:
- leaf_local: float32 [524288, 256], P(('gx', 'gy'))
Inputs may be any that keep to these rules, and one draw needn't show every extreme that they name: The 128 entries of send_boxes[s, a, j] are distinct. The entries of task_target[d, o] are distinct. `task_source`: no task of a device with gx index 0 reads rows 512 to 8703, and none of a device with gx index 1 reads the last 8192 rows. For devices d with (d // 64) even and p = d + 64, for every operator one of task_count[d, o] and task_count[p, o] exceeds 256, and the two sum to at most 512.
All inputs are finite; a program needn't handle non-finite values.
Results may differ from a plain program's by a relative error of at most 0.007.
Values may be sent and summed in bfloat16 or wider, within the bound.
A program may use at most 192 MiB of HBM per device.

v0:
```python
import jax
import jax.numpy as jnp
from jax import lax
from jax.sharding import PartitionSpec as P


def extended(shard, sides, width):
    for axis, dim in sides:
        devices, length = (lax.axis_size(axis), shard.shape[dim])
        up = [(i, (i + 1) % devices) for i in range(devices - 1)]
        down = [(j, i) for i, j in up]
        last = lax.slice_in_dim(shard, length - width, length, axis=dim)
        leading = lax.slice_in_dim(shard, 0, width, axis=dim)
        before = lax.ppermute(last, axis, up)
        after = lax.ppermute(leading, axis, down)
        shard = jnp.concatenate([before, shard, after], axis=dim)
    return shard


def translate(source_table, block_rows, block_segments, m2l_ops, segment_count):
    op_count = m2l_ops.shape[0]
    coeff_count = m2l_ops.shape[1]
    group_size = 8
    empty_row = source_table.shape[0]
    table_ext = jnp.concatenate([source_table, jnp.zeros((1, coeff_count), source_table.dtype)], 0)
    rows_grouped = block_rows.reshape(op_count // group_size, group_size, -1)
    segments_grouped = block_segments.reshape(op_count // group_size, group_size, -1)
    ops_grouped = m2l_ops.reshape(op_count // group_size, group_size, coeff_count, coeff_count)
    box_ids = jnp.arange(segment_count, dtype=jnp.int32)

    def accumulate(running, pieces):
        row_block, segment_block, op_block = pieces
        matches = segment_block[:, :, None] == box_ids[None, None, :]
        picked = jnp.sum(jnp.where(matches, row_block[:, :, None] + 1, 0), axis=1)
        inverse = jnp.where(picked == 0, empty_row, picked - 1)
        gathered = table_ext[inverse]
        added = lax.dot_general(
            gathered, op_block, (((0, 2), (0, 1)), ((), ())), preferred_element_type=jnp.float32
        )
        return (running + added, None)

    running, _ = lax.scan(
        accumulate,
        jnp.zeros((segment_count, coeff_count), jnp.float32),
        (rows_grouped, segments_grouped, ops_grouped),
    )
    return running


def body(
    leaf_multipoles, m2m_ops, m2l_ops, l2l_ops, send_boxes, task_source, task_target, task_count
):
    coeff_count = leaf_multipoles.shape[1]
    box_count = leaf_multipoles.shape[0] // 8
    leaves = leaf_multipoles.reshape(box_count, 8, coeff_count)
    parents = jnp.einsum("bcp,cpq->bq", leaves, m2m_ops, preferred_element_type=jnp.float32).astype(
        jnp.bfloat16
    )
    outgoing = parents[send_boxes[0]]
    mixed = lax.all_to_all(outgoing, "gy", split_axis=1, concat_axis=1, tiled=True)
    sides = jnp.stack([mixed[0], mixed[2]], 0)
    padded = extended(sides, (("gx", 0),), 1)
    arrived = jnp.stack([padded[0], mixed[1], padded[3]], 0)
    source_table = jnp.concatenate([parents, arrived.reshape(-1, coeff_count)], 0)
    sources = task_source[0]
    targets = task_target[0]
    counts = task_count[0]
    slot_total = sources.shape[1]
    position = jnp.arange(slot_total, dtype=jnp.int32)[None, :]
    segment = jnp.where(position < counts[:, None], targets, box_count)
    parent_local = translate(source_table, sources, segment, m2l_ops, box_count)
    parent_rounded = parent_local.astype(jnp.bfloat16)
    leaf_local = jnp.einsum(
        "bp,cpq->bcq", parent_rounded, l2l_ops, preferred_element_type=jnp.float32
    )
    return leaf_local.reshape(-1, coeff_count)


def solution(mesh):
    return jax.shard_map(
        body,
        mesh=mesh,
        in_specs=(
            P(("gx", "gy"), None),
            P(),
            P(),
            P(),
            P(("gx", "gy"), None, None, None),
            P(("gx", "gy"), None, None),
            P(("gx", "gy"), None, None),
            P(("gx", "gy"), None),
        ),
        out_specs=P(("gx", "gy"), None),
        check_vma=False,
    )
```

profile of v0, /device:TPU:1, one launch (start us, length us, event | category | flops | bytes accessed | tf_op | source)
XLA Modules:
  0.0 607.0 jit_solution(15215022823385130956)
XLA Ops:
  3.6 97.3 %gather_fusion.1 = bf16[24576,256]{1,0:T(8,128)(2,1)} fusion(bf16[512,256]{1,0:T(8,128)(2,1)S(1)} %fusion.12, s32[24576]{0:T(1024)S(1)} %broadcast_clamp_fusion.1), kind=kCustom, calls=%fused_computation.1 | custom fusion | bytes 25264128 | tf_op jit(solution)/shard_map/gather | solution.py:59
  100.9 6.4 %copy.22 = bf16[3,64,128,256]{3,2,0,1:T(8,128)(2,1)S(1)} copy(bf16[3,64,128,256]{3,2,1,0:T(8,128)(2,1)} %bitcast.65) | data formatting | bytes 25165824 | tf_op jit(solution)/shard_map/gather | solution.py:59
  107.3 158.1 %all_to_all.5 = bf16[3,64,128,256]{3,2,0,1:T(8,128)(2,1)S(1)} all-to-all(bf16[3,64,128,256]{3,2,0,1:T(8,128)(2,1)S(1)} %copy.22), channel_id=1, replica_groups=mesh['gx'=2,'gy'=64] {'gy'}, dimensions={1} | all-to-all | bytes 25165824 | tf_op jit(solution)/shard_map/all_to_all | solution.py:60
  265.4 4.8 slice_bitcast_fusion.2
  271.5 8.0 %collective-permute-start.1 = (bf16[1,64,128,256]{3,2,1,0:T(8,128)(2,1)}, bf16[1,64,128,256]{3,2,1,0:T(8,128)(2,1)}, u32[]{:S(2)}, u32[]{:S(2)}) collective-permute-start(bf16[1,64,128,256]{3,2,1,0:T(8,128)(2,1)} %get-tuple-element.134), channel_id=1, source_target_pairs={{64,0},{65,1},{66,2},{67,3},{68,4},{69,5},{70,6},{71,7},{72,8},{73... | collective-permute-start | bytes 12582920 | tf_op jit(solution)/shard_map/ppermute | solution.py:15
  281.0 3.7 collective-permute-done.1
  284.7 6.4 %pad_maximum_fusion = bf16[3,64,128,256]{3,2,1,0:T(8,128)(2,1)S(1)} fusion(bf16[1,64,128,256]{3,2,1,0:T(8,128)(2,1)} %collective-permute-done.1, bf16[1,64,128,256]{3,2,1,0:T(8,128)(2,1)} %get-tuple-element.133, bf16[1,64,128,256]{3,2,1,0:T(8,128)(2,1)} %collective-permute-done), kind=kLoop, calls=%fused_computation.16 | loop fusion | flops 12582912 | bytes 25165824 | tf_op jit(solution)/shard_map/stack | solution.py:63
  291.1 17.4 %maximum_maximum_fusion = bf16[25089,256]{1,0:T(8,128)(2,1)} fusion(bf16[24576,256]{1,0:T(8,128)(2,1)S(1)} %bitcast.66, bf16[512,256]{1,0:T(8,128)(2,1)S(1)} %fusion.12, bf16[25089]{0:T(1024)(128)(2,1)S(1)} %pad.2.clone), kind=kLoop, calls=%fused_computation.15 | loop fusion | flops 38536704 | bytes 25740802 | tf_op jit(solution)/shard_map/concatenate | solution.py:25
  308.5 292.4 %while.13 = (s32[]{:T(128)}, f32[512,256]{1,0:T(8,128)}, s32[12,8,512]{2,1,0:T(8,128)S(1)}, s32[12,8,512]{2,1,0:T(8,128)}, bf16[25089,256]{1,0:T(8,128)(2,1)}, /...) while((s32[]{:T(128)}, f32[512,256]{1,0:T(8,128)}, s32[12,8,512]{2,1,0:T(8,128)S(1)}, ...), condition=%wide.region_2.3_spmd.clone, body=%wide.region_0.2_spmd.clone.sunk | while | flops 543453184 | bytes 8618595 | solution.py:42
  310.7 19.3 %gather_fusion = bf16[4096,256]{1,0:T(8,128)(2,1)S(1)} fusion(bf16[25089,256]{1,0:T(8,128)(2,1)} %get-tuple-element.196, s32[4096]{0:T(1024)S(1)} %broadcast_clamp_fusion.3), kind=kCustom, calls=%fused_computation.clone.clone.1 | custom fusion | bytes 4210688 | tf_op jit(solution)/shard_map/while/body/eval_jaxpr/gather | solution.py:36
  334.9 19.3 %gather_fusion = bf16[4096,256]{1,0:T(8,128)(2,1)S(1)} fusion(bf16[25089,256]{1,0:T(8,128)(2,1)} %get-tuple-element.196, s32[4096]{0:T(1024)S(1)} %broadcast_clamp_fusion.3), kind=kCustom, calls=%fused_computation.clone.clone.1 | custom fusion | bytes 4210688 | tf_op jit(solution)/shard_map/while/body/eval_jaxpr/gather | solution.py:36
  359.3 19.3 %gather_fusion = bf16[4096,256]{1,0:T(8,128)(2,1)S(1)} fusion(bf16[25089,256]{1,0:T(8,128)(2,1)} %get-tuple-element.196, s32[4096]{0:T(1024)S(1)} %broadcast_clamp_fusion.3), kind=kCustom, calls=%fused_computation.clone.clone.1 | custom fusion | bytes 4210688 | tf_op jit(solution)/shard_map/while/body/eval_jaxpr/gather | solution.py:36
  383.7 19.3 %gather_fusion = bf16[4096,256]{1,0:T(8,128)(2,1)S(1)} fusion(bf16[25089,256]{1,0:T(8,128)(2,1)} %get-tuple-element.196, s32[4096]{0:T(1024)S(1)} %broadcast_clamp_fusion.3), kind=kCustom, calls=%fused_computation.clone.clone.1 | custom fusion | bytes 4210688 | tf_op jit(solution)/shard_map/while/body/eval_jaxpr/gather | solution.py:36
  408.0 19.3 %gather_fusion = bf16[4096,256]{1,0:T(8,128)(2,1)S(1)} fusion(bf16[25089,256]{1,0:T(8,128)(2,1)} %get-tuple-element.196, s32[4096]{0:T(1024)S(1)} %broadcast_clamp_fusion.3), kind=kCustom, calls=%fused_computation.clone.clone.1 | custom fusion | bytes 4210688 | tf_op jit(solution)/shard_map/while/body/eval_jaxpr/gather | solution.py:36
  427.3 2.9 fusion.28
  432.4 19.3 %gather_fusion = bf16[4096,256]{1,0:T(8,128)(2,1)S(1)} fusion(bf16[25089,256]{1,0:T(8,128)(2,1)} %get-tuple-element.196, s32[4096]{0:T(1024)S(1)} %broadcast_clamp_fusion.3), kind=kCustom, calls=%fused_computation.clone.clone.1 | custom fusion | bytes 4210688 | tf_op jit(solution)/shard_map/while/body/eval_jaxpr/gather | solution.py:36
  456.8 19.3 %gather_fusion = bf16[4096,256]{1,0:T(8,128)(2,1)S(1)} fusion(bf16[25089,256]{1,0:T(8,128)(2,1)} %get-tuple-element.196, s32[4096]{0:T(1024)S(1)} %broadcast_clamp_fusion.3), kind=kCustom, calls=%fused_computation.clone.clone.1 | custom fusion | bytes 4210688 | tf_op jit(solution)/shard_map/while/body/eval_jaxpr/gather | solution.py:36
  481.2 19.3 %gather_fusion = bf16[4096,256]{1,0:T(8,128)(2,1)S(1)} fusion(bf16[25089,256]{1,0:T(8,128)(2,1)} %get-tuple-element.196, s32[4096]{0:T(1024)S(1)} %broadcast_clamp_fusion.3), kind=kCustom, calls=%fused_computation.clone.clone.1 | custom fusion | bytes 4210688 | tf_op jit(solution)/shard_map/while/body/eval_jaxpr/gather | solution.py:36
  500.5 2.9 fusion.28
  505.6 19.3 %gather_fusion = bf16[4096,256]{1,0:T(8,128)(2,1)S(1)} fusion(bf16[25089,256]{1,0:T(8,128)(2,1)} %get-tuple-element.196, s32[4096]{0:T(1024)S(1)} %broadcast_clamp_fusion.3), kind=kCustom, calls=%fused_computation.clone.clone.1 | custom fusion | bytes 4210688 | tf_op jit(solution)/shard_map/while/body/eval_jaxpr/gather | solution.py:36
  529.9 19.3 %gather_fusion = bf16[4096,256]{1,0:T(8,128)(2,1)S(1)} fusion(bf16[25089,256]{1,0:T(8,128)(2,1)} %get-tuple-element.196, s32[4096]{0:T(1024)S(1)} %broadcast_clamp_fusion.3), kind=kCustom, calls=%fused_computation.clone.clone.1 | custom fusion | bytes 4210688 | tf_op jit(solution)/shard_map/while/body/eval_jaxpr/gather | solution.py:36
  554.3 19.3 %gather_fusion = bf16[4096,256]{1,0:T(8,128)(2,1)S(1)} fusion(bf16[25089,256]{1,0:T(8,128)(2,1)} %get-tuple-element.196, s32[4096]{0:T(1024)S(1)} %broadcast_clamp_fusion.3), kind=kCustom, calls=%fused_computation.clone.clone.1 | custom fusion | bytes 4210688 | tf_op jit(solution)/shard_map/while/body/eval_jaxpr/gather | solution.py:36
  578.7 19.3 %gather_fusion = bf16[4096,256]{1,0:T(8,128)(2,1)S(1)} fusion(bf16[25089,256]{1,0:T(8,128)(2,1)} %get-tuple-element.196, s32[4096]{0:T(1024)S(1)} %broadcast_clamp_fusion.3), kind=kCustom, calls=%fused_computation.clone.clone.1 | custom fusion | bytes 4210688 | tf_op jit(solution)/shard_map/while/body/eval_jaxpr/gather | solution.py:36
  602.6 4.4 copy.38
  (88 shorter events, 62.8 us)
Async XLA Ops:
  0.0 600.8 %copy-start = (bf16[8,256,256]{2,1,0:T(8,128)(2,1)S(1)}, bf16[8,256,256]{2,1,0:T(8,128)(2,1)}, u32[]{:S(2)}) copy-start(bf16[8,256,256]{2,1,0:T(8,128)(2,1)} %param.13) | copy-start | bytes 3145732
  265.4 14.7 %copy-start.2 = (s32[1,96]{1,0:T(1,128)S(1)}, s32[1,96]{1,0:T(1,128)}, u32[]{:S(2)}) copy-start(s32[1,96]{1,0:T(1,128)} %param.17) | copy-start | bytes 1156
  265.4 15.5 %copy-start.1 = (s32[1,96,512]{2,1,0:T(8,128)S(1)}, s32[1,96,512]{2,1,0:T(8,128)}, u32[]{:S(2)}) copy-start(s32[1,96,512]{2,1,0:T(8,128)} %param.16) | copy-start | bytes 589828
  270.2 10.8 %collective-permute-start = (bf16[1,64,128,256]{3,2,1,0:T(8,128)(2,1)}, bf16[1,64,128,256]{3,2,1,0:T(8,128)(2,1)}, u32[]{:S(2)}, u32[]{:S(2)}) collective-permute-start(bf16[1,64,128,256]{3,2,1,0:T(8,128)(2,1)} %get-tuple-element.132), channel_id=1, source_target_pairs={{0,64},{1,65},{2,66},{3,67},{4,68},{5,69},{6,70},{7,71},{8,72},{9,... | collective-permute-start | bytes 12582920 | tf_op jit(solution)/shard_map/ppermute | solution.py:14
  271.5 13.2 %collective-permute-start.1 = (bf16[1,64,128,256]{3,2,1,0:T(8,128)(2,1)}, bf16[1,64,128,256]{3,2,1,0:T(8,128)(2,1)}, u32[]{:S(2)}, u32[]{:S(2)}) collective-permute-start(bf16[1,64,128,256]{3,2,1,0:T(8,128)(2,1)} %get-tuple-element.134), channel_id=1, source_target_pairs={{64,0},{65,1},{66,2},{67,3},{68,4},{69,5},{70,6},{71,7},{72,8},{73... | collective-permute-start | bytes 12582920 | tf_op jit(solution)/shard_map/ppermute | solution.py:15
where the time goes:
time: 609 us; the launch traced here: 607 us
  local copies, waits for them, and re-layouts  345 us (57%)
  blocking collectives  158 us (26%)
  other arithmetic  51.6 us (8%)
  matrix products  38.6 us (6%)
  starting transfers between devices  9.3 us (2%)
    gather x12, local copies, waits for them, and re-layouts, accumulate(): gathered = table_ext[inverse]  231 us
    all_to_all x1, blocking collectives, body(): lax.all_to_all(outgoing, 'gy', split_axis=1, concat_axis=1, tiled=True)  158 us
    gather x2, local copies, waits for them, and re-layouts, body(): outgoing = parents[send_boxes[0]]  104 us
    dot_general x12, matrix products, accumulate(): lax.dot_general(gathered, op_block, (((0, 2), (0, 1)), ((), ())), preferr...  34.3 us
    concatenate x1, other arithmetic, translate(): jnp.concatenate([source_table, jnp.zeros((1, coeff_count), source_table.d...  17.4 us
    reduce_sum x12, other arithmetic, accumulate(): picked = jnp.sum(jnp.where(matches, row_block[:, :, None] + 1, 0), axis=1)  17.3 us
  transfers between devices with their start and end apart: 2, of which 1 were waited for; matrix products, arithmetic and copies ran while one was open for 0% of the time, Pallas kernels for 0%

commit v1 on v0

v1 whole, which is shorter than its diff:
```python
import jax
import jax.numpy as jnp
from jax import lax
from jax.experimental import pallas as pl
from jax.experimental.pallas import tpu as pltpu
from jax.sharding import PartitionSpec as P

CHUNK = 128


def m2l_kernel(ops, chunks_per_op, src_ref, nch_ref, tgt_ref, tab_hbm, op_hbm, out_ref,
               tab_ref, op_ref, xa_ref, xb_ref, acc_ref, list_ref, sem):
    coeffs = acc_ref.shape[1]
    boxes = acc_ref.shape[0]
    load_table = pltpu.make_async_copy(tab_hbm, tab_ref, sem.at[0])
    load_table.start()
    load_ops = pltpu.make_async_copy(op_hbm, op_ref, sem.at[1])
    load_ops.start()
    acc_ref[...] = jnp.zeros_like(acc_ref)

    def fill(o, pos):
        n = nch_ref[o]
        for c in range(chunks_per_op):
            list_ref[pos] = o * chunks_per_op + c
            pos = pos + jnp.where(c < n, 1, 0)
        return pos

    total = lax.fori_loop(0, ops, fill, 0)
    for i in range(8):
        list_ref[total + i] = ops * chunks_per_op
    load_table.wait()
    load_ops.wait()

    def gather(it, x_ref):
        for h in range(2):
            b = list_ref[2 * it + h] * CHUNK
            for i in range(CHUNK):
                x_ref[h * CHUNK + i] = tab_ref[src_ref[b + i]].astype(jnp.float32)

    def compute(it, x_ref):
        x2 = x_ref.reshape(4 * CHUNK, 128)
        ys, ps = [], []
        rows = lax.broadcasted_iota(jnp.int32, (boxes, CHUNK), 0)
        for h in range(2):
            ch = list_ref[2 * it + h]
            lo = x2[pl.ds(h * 2 * CHUNK, CHUNK, stride=2), :].astype(jnp.bfloat16)
            hi = x2[pl.ds(h * 2 * CHUNK + 1, CHUNK, stride=2), :].astype(jnp.bfloat16)
            xx = jnp.concatenate([lo, hi], axis=1)
            o = jnp.minimum(lax.div(ch, chunks_per_op), ops - 1)
            w = op_ref[pl.ds(pl.multiple_of(o * coeffs, coeffs), coeffs), :]
            ys.append(jnp.dot(xx, w, preferred_element_type=jnp.float32).astype(jnp.bfloat16))
            t = tgt_ref[pl.ds(ch, 1), :]
            ps.append(jnp.where(rows == t, 1.0, 0.0).astype(jnp.bfloat16))
        acc_ref[...] += jnp.dot(
            jnp.concatenate(ps, axis=1), jnp.concatenate(ys, axis=0),
            preferred_element_type=jnp.float32,
        )

    gather(0, xa_ref)

    @pl.loop(0, lax.div(total + 3, 4))
    def _(j):
        gather(2 * j + 1, xb_ref)
        compute(2 * j, xa_ref)
        gather(2 * j + 2, xa_ref)
        compute(2 * j + 1, xb_ref)

    out_ref[...] = acc_ref[...].astype(out_ref.dtype)


def m2l(table, src, tgt, counts, m2l_ops, boxes):
    ops, slots = src.shape
    coeffs = m2l_ops.shape[1]
    rows = table.shape[0]
    chunks_per_op = slots // CHUNK
    position = jnp.arange(slots, dtype=jnp.int32)[None, :]
    tgt = jnp.where(position < counts[:, None], tgt, -1)
    tgt = jnp.concatenate([tgt, jnp.full((8, slots), -1, jnp.int32)], 0)
    tgt = tgt.reshape(-1, CHUNK)
    src = jnp.concatenate([src.reshape(-1), jnp.zeros((slots,), jnp.int32)], 0)
    nch = (counts + (CHUNK - 1)) // CHUNK
    smem = pl.BlockSpec(memory_space=pltpu.SMEM)
    vmem = pl.BlockSpec(memory_space=pltpu.VMEM)
    anym = pl.BlockSpec(memory_space=pl.ANY)

    def kern(*refs):
        m2l_kernel(ops, chunks_per_op, *refs)

    return pl.pallas_call(
        kern,
        in_specs=[smem, smem, vmem, anym, anym],
        out_specs=vmem,
        out_shape=jax.ShapeDtypeStruct((boxes, coeffs), jnp.bfloat16),
        scratch_shapes=[
            pltpu.VMEM((rows, 2, 128), jnp.bfloat16),
            pltpu.VMEM((ops * coeffs, coeffs), jnp.bfloat16),
            pltpu.VMEM((2 * CHUNK, 2, 128), jnp.float32),
            pltpu.VMEM((2 * CHUNK, 2, 128), jnp.float32),
            pltpu.VMEM((boxes, coeffs), jnp.float32),
            pltpu.SMEM((ops * chunks_per_op + 16,), jnp.int32),
            pltpu.SemaphoreType.DMA((2,)),
        ],
        compiler_params=pltpu.CompilerParams(vmem_limit_bytes=50 << 20),
        name="m2l",
    )(src, nch, tgt, table, m2l_ops.reshape(ops * coeffs, coeffs))


def body(
    leaf_multipoles, m2m_ops, m2l_ops, l2l_ops, send_boxes, task_source, task_target, task_count
):
    coeff_count = leaf_multipoles.shape[1]
    box_count = leaf_multipoles.shape[0] // 8
    column = lax.axis_index("gx")
    leaves = leaf_multipoles.reshape(box_count, 8, coeff_count)
    parents = jnp.einsum("bcp,cpq->bq", leaves, m2m_ops, preferred_element_type=jnp.float32).astype(
        jnp.bfloat16
    )
    boxes = send_boxes[0]
    cap = boxes.shape[-1]
    peers = boxes.shape[1]
    other = jnp.where(column == 0, boxes[2], boxes[0])
    lists = jnp.stack([boxes[1], other], 0)
    outgoing = parents[lists]
    mixed = lax.all_to_all(outgoing, "gy", split_axis=1, concat_axis=1, tiled=True)
    crossed = lax.ppermute(mixed[1], "gx", [(0, 1), (1, 0)])
    table = jnp.concatenate(
        [parents, mixed[0].reshape(-1, coeff_count), crossed.reshape(-1, coeff_count)], 0
    )
    rows = table.shape[0]
    sources = task_source[0]
    block = peers * cap
    own = jnp.logical_and(sources >= box_count, sources < box_count + block)
    shifted = jnp.where(
        jnp.logical_and(column == 1, own), sources + block, sources - block
    )
    src = jnp.where(sources < box_count, sources, shifted)
    src = jnp.clip(src, 0, rows - 1)
    parent_rounded = m2l(
        table.reshape(rows, 2, 128), src, task_target[0], task_count[0], m2l_ops, box_count
    )
    leaf_local = jnp.einsum(
        "bp,cpq->bcq", parent_rounded, l2l_ops, preferred_element_type=jnp.float32
    )
    return leaf_local.reshape(-1, coeff_count)


def solution(mesh):
    return jax.shard_map(
        body,
        mesh=mesh,
        in_specs=(
            P(("gx", "gy"), None),
            P(),
            P(),
            P(),
            P(("gx", "gy"), None, None, None),
            P(("gx", "gy"), None, None),
            P(("gx", "gy"), None, None),
            P(("gx", "gy"), None),
        ),
        out_specs=P(("gx", "gy"), None),
        check_vma=False,
    )
```

time: 609 us -> 331 us (0.54)
  local copies, waits for them, and re-layouts: 345 us -> 95.4 us
  Pallas kernels: 0 us -> 63.7 us
  blocking collectives: 158 us -> 110 us
  matrix products: 38.6 us -> 3.38 us
  starting transfers between devices: 9.3 us -> 2.22 us
    gather x14 -> x2, local copies, waits for them, and re-layouts: 335 us -> 72.9 us  [body(): outgoing = parents[lists]]
    pallas_call x0 -> x1, Pallas kernels: none -> 63.7 us  [m2l(): pl.pallas_call(kern, in_specs=[smem, smem, vmem, anym, anym], out_specs=v...]
    all_to_all x1, blocking collectives: 158 us -> 110 us  [body(): lax.all_to_all(outgoing, 'gy', split_axis=1, concat_axis=1, tiled=True)]
    concatenate x1, other arithmetic: 17.4 us -> 53.9 us  [body(): jnp.concatenate([parents, mixed[0].reshape(-1, coeff_count), crossed.resh...]
    dot_general x12 -> x0, matrix products: 34.3 us -> none  [accumulate(): lax.dot_general(gathered, op_block, (((0, 2), (0, 1)), ((), ())), preferr...]
    reduce_sum x12 -> x0, other arithmetic: 17.3 us -> none  [accumulate(): picked = jnp.sum(jnp.where(matches, row_block[:, :, None] + 1, 0), axis=1)]
    concatenate x1 -> x5, local copies, waits for them, and re-layouts: 0.01 us -> 14 us  [the longest x3 14 us: body(): jnp.concatenate([parents, mixed[0].reshape(-1, coeff_count), crossed.resh...]
    add x12 -> x0, other arithmetic: 8.65 us -> none  [accumulate(): picked = jnp.sum(jnp.where(matches, row_block[:, :, None] + 1, 0), axis=1)]
  transfers between devices with their start and end apart: 2 -> 1, of which waited for: 1 -> 0; matrix products, arithmetic and copies ran while one was open for 0% -> 2% of each run, Pallas kernels for 0% -> 0%
where the time goes in v1:
time: 331 us; the launch traced here: 330 us
  blocking collectives  110 us (33%)
  local copies, waits for them, and re-layouts  95.4 us (29%)
  Pallas kernels  63.7 us (19%)
  other arithmetic  55 us (17%)
  matrix products  3.38 us (1%)
    all_to_all x1, blocking collectives, body(): lax.all_to_all(outgoing, 'gy', split_axis=1, concat_axis=1, tiled=True)  110 us
    gather x2, local copies, waits for them, and re-layouts, body(): outgoing = parents[lists]  72.9 us
    pallas_call x1, Pallas kernels, m2l(): pl.pallas_call(kern, in_specs=[smem, smem, vmem, anym, anym], out_specs=v...  63.7 us
    concatenate x1, other arithmetic, body(): jnp.concatenate([parents, mixed[0].reshape(-1, coeff_count), crossed.resh...  53.9 us
    concatenate x3, local copies, waits for them, and re-layouts, body(): jnp.concatenate([parents, mixed[0].reshape(-1, coeff_count), crossed.resh...  14 us
  transfers between devices with their start and end apart: 1, of which 0 were waited for; matrix products, arithmetic and copies ran while one was open for 2% of the time, Pallas kernels for 0%

profile of v1, /device:TPU:1, one launch (start us, length us, event | category | flops | bytes accessed | tf_op | source)
XLA Modules:
  0.0 330.1 jit_solution(13644843576358499769)
XLA Ops:
  0.0 0.0 copy-start
  0.0 0.9 slice_bitcast_fusion.1
  0.9 2.7 fusion.5
  3.6 0.1 copy.21
  3.7 65.2 %gather_fusion = bf16[16384,256]{1,0:T(8,128)(2,1)} fusion(bf16[512,256]{1,0:T(8,128)(2,1)S(1)} %copy.21, s32[16384]{0:T(1024)S(1)} %broadcast_clamp_fusion), kind=kCustom, calls=%fused_computation | custom fusion | bytes 16842752 | tf_op jit(solution)/shard_map/gather | solution.py:123
  68.9 7.7 %copy.22 = bf16[2,64,128,256]{3,2,0,1:T(8,128)(2,1)} copy(bf16[2,64,128,256]{3,2,1,0:T(8,128)(2,1)} %bitcast.33) | data formatting | bytes 16777216 | tf_op jit(solution)/shard_map/gather | solution.py:123
  76.7 110.3 %all_to_all.5 = bf16[2,64,128,256]{3,2,0,1:T(8,128)(2,1)S(1)} all-to-all(bf16[2,64,128,256]{3,2,0,1:T(8,128)(2,1)} %copy.22), channel_id=1, replica_groups=mesh['gx'=2,'gy'=64] {'gy'}, dimensions={1} | all-to-all | bytes 16777216 | tf_op jit(solution)/shard_map/all_to_all | solution.py:124
  187.0 3.8 %fusion.11 = (bf16[1,64,128,256]{3,2,0,1:T(8,128)(2,1)}, bf16[64,128,256]{2,1,0:T(8,128)(2,1)}) fusion(bf16[2,64,128,256]{3,2,0,1:T(8,128)(2,1)S(1)} %all_to_all.5), kind=kLoop, calls=%fused_computation.22 | loop fusion | bytes 16777216 | tf_op jit(solution)/shard_map/slice | solution.py:127
  190.8 2.2 collective-permute-start
  193.0 0.2 copy.25
  193.2 0.0 copy-done.1
  193.2 0.1 copy.26
  193.3 0.1 fusion.10
  193.4 0.0 copy-done.2
  193.4 0.0 copy-done.3
  193.4 0.1 bitcast_select_fusion
  193.6 6.9 %concatenate.38 = bf16[8192,2,128]{2,1,0:T(2,128)(2,1)} reshape(bf16[1,64,128,256]{3,2,0,1:T(8,128)(2,1)} %get-tuple-element.5) | data formatting | bytes 8388608 | tf_op jit(solution)/shard_map/concatenate | solution.py:126
  200.5 0.0 collective-permute-done
  200.5 6.9 %concatenate.39 = bf16[8192,2,128]{2,1,0:T(2,128)(2,1)} reshape(bf16[64,128,256]{2,1,0:T(8,128)(2,1)} %collective-permute-done) | data formatting | bytes 8388608 | tf_op jit(solution)/shard_map/concatenate | solution.py:126
  207.4 53.9 %pad_maximum_fusion.refs_3_ = bf16[16896,2,128]{2,1,0:T(2,128)(2,1)} fusion(bf16[8192,2,128]{2,1,0:T(2,128)(2,1)} %concatenate.39, bf16[8192,2,128]{2,1,0:T(2,128)(2,1)} %concatenate.38, bf16[512,2,128]{2,1,0:T(2,128)(2,1)S(1)} %copy.25), kind=kLoop, calls=%fused_computation.1 | loop fusion | flops 8650752 | bytes 17301504 | tf_op jit(solution)/shard_map/concatenate | solution.py:126
  261.3 63.7 %m2l.1 = bf16[512,256]{1,0:T(8,128)(2,1)S(1)} custom-call(s32[49664]{0:T(1024)S(1)} %concatenate.35.refs_0_, s32[96]{0:T(128)S(1)} %and_select_fusion.refs_1_, s32[416,128]{1,0:T(8,128)S(1)} %reshape.137.refs_2_, bf16[16896,2,128]{2,1,0:T(2,128)(2,1)} %pad_maximum_fusion.refs_3_, bf16[24576,256]{1,0:T(8,128)(2,1)} %bitcast.34), custom_call_target="tpu_custom_call" | custom-call | tf_op jit(solution)/shard_map/m2l/pallas_call | solution.py:89
  324.9 0.0 copy-done
  324.9 0.7 fusion.8
  325.6 4.4 %copy.34 = f32[512,8,256]{2,1,0:T(8,128)} copy(f32[512,8,256]{2,0,1:T(8,128)S(1)} %fusion.8) | data formatting | bytes 8388608 | tf_op jit(solution)/shard_map/bp,cpq->bcq/dot_general | solution.py:141
  (9 shorter events, 0.1 us)
Async XLA Ops:
  0.0 324.9 %copy-start = (bf16[8,256,256]{2,1,0:T(8,128)(2,1)S(1)}, bf16[8,256,256]{2,1,0:T(8,128)(2,1)}, u32[]{:S(2)}) copy-start(bf16[8,256,256]{2,1,0:T(8,128)(2,1)} %param.11) | copy-start | bytes 3145732
  186.9 6.2 %copy-start.1 = (s32[1,96,512]{2,1,0:T(8,128)S(1)}, s32[1,96,512]{2,1,0:T(8,128)}, u32[]{:S(2)}) copy-start(s32[1,96,512]{2,1,0:T(8,128)} %param.13) | copy-start | bytes 589828
  187.0 6.4 %copy-start.2 = (s32[1,96,512]{2,1,0:T(8,128)S(1)}, s32[1,96,512]{2,1,0:T(8,128)}, u32[]{:S(2)}) copy-start(s32[1,96,512]{2,1,0:T(8,128)} %param.14) | copy-start | bytes 589828
  187.0 6.5 %copy-start.3 = (s32[1,96]{1,0:T(1,128)S(1)}, s32[1,96]{1,0:T(1,128)}, u32[]{:S(2)}) copy-start(s32[1,96]{1,0:T(1,128)} %param.15) | copy-start | bytes 1156
  190.8 9.7 %collective-permute-start = (bf16[64,128,256]{2,1,0:T(8,128)(2,1)}, bf16[64,128,256]{2,1,0:T(8,128)(2,1)}, u32[]{:S(2)}, u32[]{:S(2)}) collective-permute-start(bf16[64,128,256]{2,1,0:T(8,128)(2,1)} %get-tuple-element.6), channel_id=1, source_target_pairs={{0,64},{64,0},{1,65},{65,1},{2,66},{66,2},{3,67},{67,3},{4,68},{68... | collective-permute-start | bytes 12582920 | tf_op jit(solution)/shard_map/ppermute | solution.py:125

commit v2 on v1

--- a/solution.py
+++ b/solution.py
@@ -6,15 +6,222 @@
 from jax.sharding import PartitionSpec as P
 
 CHUNK = 128
-
-
-def m2l_kernel(ops, chunks_per_op, src_ref, nch_ref, tgt_ref, tab_hbm, op_hbm, out_ref,
+SIDE = 4
+UNROLL = 16
+
+INTERNAL = (0, 12, 4, 48, 28, 7, 49, 52, 29, 11, 6, 23, 45, 10, 22, 41, 46, 47)
+PARENT = (-1, 0, 6, 7, 0, 6, 7, 4, 12, 10, 6, 7, 0, 29, 10, 12, 0, 29, 22, 23, 4, 22, 23, 7, 28, 41, 22, 11, 12, 28, 29, 47, 48, 49, 46, 47, 52, 41, 22, 23, 41, 45, 41, 47, 45, 29, 45, 46, 0, 48, 49, 48, 48, 52, 6, 7, 52, 41, 10, 11, 12, 49, 46, 47)
+PLAN = (
+    (0, 0, 0), (0, 0, 1), (1, 0, 0), (1, 0, 1), (1, 0, 16), (0, 12, 0), (0, 4, 0), (0, 48, 0),
+    (0, 12, 1), (0, 4, 1), (0, 48, 1), (1, 12, 12), (1, 12, 8), (1, 12, 15), (1, 12, 60),
+    (1, 4, 4), (1, 4, 20), (0, 28, 0), (0, 7, 0), (0, 49, 0), (1, 48, 48), (1, 48, 32),
+    (1, 48, 51), (0, 52, 0), (0, 28, 1), (0, 7, 1), (0, 49, 1), (1, 28, 28), (1, 28, 24),
+    (1, 7, 7), (1, 7, 3), (1, 7, 55), (0, 52, 1), (1, 49, 49), (1, 49, 33), (1, 49, 50),
+    (1, 49, 61), (1, 52, 52), (1, 52, 36), (0, 29, 0), (1, 52, 53), (1, 52, 56), (0, 11, 0),
+    (0, 29, 1), (0, 6, 0), (0, 23, 0), (1, 29, 29), (1, 29, 13), (1, 29, 17), (1, 29, 30),
+    (0, 11, 1), (1, 11, 11), (1, 11, 27), (1, 11, 59), (0, 23, 1), (1, 23, 23), (1, 23, 19),
+    (1, 23, 39), (0, 45, 0), (0, 6, 1), (1, 6, 6), (1, 6, 2), (1, 6, 5), (1, 6, 54), (0, 10, 0),
+    (0, 45, 1), (0, 22, 0), (1, 45, 45), (1, 45, 44), (0, 41, 0), (0, 46, 0), (0, 22, 1),
+    (1, 22, 22), (1, 22, 18), (1, 22, 21), (1, 22, 26), (1, 22, 38), (0, 10, 1), (1, 10, 10),
+    (1, 10, 9), (1, 10, 14), (1, 10, 58), (0, 46, 1), (1, 46, 46), (1, 46, 34), (1, 46, 62),
+    (0, 41, 1), (1, 41, 41), (1, 41, 25), (1, 41, 37), (0, 47, 0), (1, 41, 40), (1, 41, 42),
+    (1, 41, 57), (0, 47, 1), (1, 47, 47), (1, 47, 31), (1, 47, 35), (1, 47, 43), (1, 47, 63),
+)
+
+PAD = 4
+
+
+def list_layout():
+    groups, order, pos = {}, [], {}
+    for o in INTERNAL:
+        members = [o] + [c for c in range(len(PARENT)) if PARENT[c] == o and c not in INTERNAL]
+        start = len(order)
+        for c in members:
+            pos[c] = len(order)
+            order.append(c)
+        while len(order) % PAD:
+            order.append(o)
+        groups[o] = (start, len(order) - start)
+    return groups, order, pos
+
+
+def torus_add(base, offset, sign=1):
+    parts = []
+    for weight in (SIDE * SIDE, SIDE, 1):
+        a = lax.rem(lax.div(base, weight), SIDE)
+        b = (offset // weight) % SIDE
+        if sign < 0:
+            b = (SIDE - b) % SIDE
+        parts.append(lax.rem(a + b, SIDE) * weight)
+    return parts[0] + parts[1] + parts[2]
+
+
+def comm_kernel(idx_in, own_block, ghost_own, ghost_other, *scratch):
+    blocks = dict(zip(INTERNAL, (own_block,) + scratch[: len(INTERNAL) - 1]))
+    scratch = scratch[len(INTERNAL) - 1 :]
+    (land, idx, stage_own, stage_other, full_send, full_recv, idx_send, idx_recv, idx_load,
+     own_send, own_recv, own_local, other_send, other_recv) = scratch
+    groups, order, pos = list_layout()
+    slot = {o: i for i, o in enumerate(INTERNAL)}
+    peers = ghost_own.shape[0]
+    cap = ghost_own.shape[1]
+    half_rows = own_block.shape[0] // 2
+    pair = 2 * cap
+    me_u = lax.axis_index("gx")
+    me_v = lax.axis_index("gy")
+    ready = pltpu.get_barrier_semaphore()
+
+    def mesh_id(offset, side=0, sign=1):
+        column = me_u if side == 0 else 1 - me_u
+        return (column, torus_add(me_v, offset, sign))
+
+    near = [s * w for w in (SIDE * SIDE, SIDE, 1) for s in (1, SIDE - 1)]
+    sends = [(o, 0) for o in sorted(set(near) | set(INTERNAL[1:]))]
+    sends += [(o, 1) for o in [0] + near]
+    for o, side in sends:
+        pl.semaphore_signal(ready, inc=1, device_id=mesh_id(o, side, -1),
+                            device_id_type=pl.DeviceIdType.MESH)
+    pl.semaphore_wait(ready, len(sends))
+
+    def remote(src, dst, send, recv, target):
+        return pltpu.make_async_remote_copy(
+            src_ref=src, dst_ref=dst, send_sem=send, recv_sem=recv, device_id=target,
+            device_id_type=pl.DeviceIdType.MESH,
+        )
+
+    def full_copy(child, half):
+        parent = PARENT[child]
+        rows = pl.ds(half * half_rows, half_rows)
+        step = torus_step(parent, child)
+        k = (slot[child] - 1) * 2 + half
+        return remote(blocks[parent].at[rows], blocks[child].at[rows], full_send.at[k],
+                      full_recv.at[k], mesh_id(step))
+
+    def idx_copy(o):
+        start, n = groups[o]
+        part = pl.ds(start * pair, n * pair)
+        k = slot[o] - 1
+        return remote(idx_in.at[part], land.at[part], idx_send.at[k], idx_recv.at[k], mesh_id(o))
+
+    def idx_local(o):
+        start, n = groups[o]
+        part = pl.ds(start * pair, n * pair)
+        src = idx_in if o == 0 else land
+        return pltpu.make_async_copy(src.at[part], idx.at[part], idx_load.at[slot[o]])
+
+    children = {o: [c for c in INTERNAL if PARENT[c] == o] for o in INTERNAL}
+    loaded = set()
+    for kind, o, arg in PLAN:
+        if kind == 0:
+            if o == 0:
+                if arg == 0:
+                    idx_local(0).start()
+            else:
+                full_copy(o, arg).wait_recv()
+            for c in children[o]:
+                full_copy(c, arg).start()
+            if o == 0 and arg == 1:
+                for c in INTERNAL[1:]:
+                    idx_copy(c).start()
+            if o != 0 and arg == 1:
+                idx_copy(o).wait_recv()
+                idx_local(o).start()
+            continue
+        if o not in loaded:
+            idx_local(o).wait()
+            loaded.add(o)
+        block = blocks[o]
+        p = pos[arg]
+        for h, stage in ((0, stage_own), (1, stage_other)):
+
+            def pick(g, carry, block=block, stage=stage, h=h, p=p):
+                b = p * pair + h * cap + g * UNROLL
+                rows = [block[idx[b + i]] for i in range(UNROLL)]
+                for i in range(UNROLL):
+                    stage[p, g * UNROLL + i] = rows[i]
+                return carry
+
+            lax.fori_loop(0, cap // UNROLL, pick, 0)
+        owner = torus_add(me_v, o, -1)
+        step = torus_step(o, arg) if arg != o else 0
+        if arg == o:
+            pltpu.make_async_copy(stage_own.at[p], ghost_own.at[owner], own_local).start()
+        else:
+            remote(stage_own.at[p], ghost_own.at[owner], own_send, own_recv, mesh_id(step)).start()
+        remote(stage_other.at[p], ghost_other.at[owner], other_send, other_recv,
+               mesh_id(step, 1)).start()
+
+    here = (1 - me_u, me_v)
+    inner = len(INTERNAL)
+    part = ghost_own.at[pl.ds(0, peers - inner)]
+    remote(part, part, own_send, own_recv, here).wait_recv()
+    remote(ghost_other, ghost_other, other_send, other_recv, here).wait_recv()
+    remote(part, part, own_send, own_recv, here).wait_send()
+    remote(ghost_other, ghost_other, other_send, other_recv, here).wait_send()
+    part = ghost_own.at[pl.ds(0, inner)]
+    pltpu.make_async_copy(part, part, own_local).wait()
+    for c in INTERNAL[1:]:
+        idx_copy(c).wait_send()
+        for half in range(2):
+            full_copy(c, half).wait_send()
+
+
+def torus_step(a, b):
+    step = 0
+    for weight in (SIDE * SIDE, SIDE, 1):
+        step += (((b // weight) - (a // weight)) % SIDE) * weight
+    return step
+
+
+def exchange(parents, lists):
+    _, peers, cap = lists.shape
+    boxes, coeffs = parents.shape
+    groups, order, pos = list_layout()
+    me_v = lax.axis_index("gy")
+    dest = jnp.stack([torus_add(me_v, o) for o in order])
+    idx = jnp.transpose(lists, (1, 0, 2))[dest].reshape(-1)
+    inner = len(INTERNAL)
+    dma = pltpu.SemaphoreType.DMA
+    anym = pl.BlockSpec(memory_space=pl.ANY)
+    vmem = pl.BlockSpec(memory_space=pltpu.VMEM)
+    ghost = jax.ShapeDtypeStruct((peers, cap, 2, coeffs // 2), parents.dtype)
+    return pl.pallas_call(
+        comm_kernel,
+        in_specs=[vmem, vmem],
+        out_specs=[anym, anym],
+        out_shape=[ghost, ghost],
+        scratch_shapes=[pltpu.VMEM((boxes, 2, coeffs // 2), parents.dtype)] * (inner - 1)
+        + [
+            pltpu.VMEM(idx.shape, jnp.int32),
+            pltpu.SMEM(idx.shape, jnp.int32),
+            pltpu.VMEM((len(order), cap, 2, coeffs // 2), parents.dtype),
+            pltpu.VMEM((len(order), cap, 2, coeffs // 2), parents.dtype),
+            dma((2 * inner - 2,)),
+            dma((2 * inner - 2,)),
+            dma((inner - 1,)),
+            dma((inner - 1,)),
+            dma((inner,)),
+            dma, dma, dma, dma, dma,
+        ],
+        compiler_params=pltpu.CompilerParams(
+            collective_id=0, has_side_effects=True, vmem_limit_bytes=40 << 20
+        ),
+        name="exchange",
+    )(idx, parents.reshape(boxes, 2, coeffs // 2))
+
+
+def m2l_kernel(ops, chunks_per_op, src_ref, nch_ref, tgt_ref, par_hbm, own_hbm, other_hbm, op_hbm, out_ref,
                tab_ref, op_ref, xa_ref, xb_ref, acc_ref, list_ref, sem):
     coeffs = acc_ref.shape[1]
     boxes = acc_ref.shape[0]
-    load_table = pltpu.make_async_copy(tab_hbm, tab_ref, sem.at[0])
-    load_table.start()
-    load_ops = pltpu.make_async_copy(op_hbm, op_ref, sem.at[1])
+    loads = []
+    first = 0
+    for i, part in enumerate((par_hbm, own_hbm, other_hbm)):
+        n = part.shape[0]
+        loads.append(pltpu.make_async_copy(part, tab_ref.at[pl.ds(first, n)], sem.at[1 + i]))
+        loads[-1].start()
+        first += n
+    load_ops = pltpu.make_async_copy(op_hbm, op_ref, sem.at[0])
     load_ops.start()
     acc_ref[...] = jnp.zeros_like(acc_ref)
 
@@ -28,7 +235,8 @@
     total = lax.fori_loop(0, ops, fill, 0)
     for i in range(8):
         list_ref[total + i] = ops * chunks_per_op
-    load_table.wait()
+    for load in loads:
+        load.wait()
     load_ops.wait()
 
     def gather(it, x_ref):
@@ -68,10 +276,11 @@
     out_ref[...] = acc_ref[...].astype(out_ref.dtype)
 
 
-def m2l(table, src, tgt, counts, m2l_ops, boxes):
+def m2l(parents, ghosts, src, tgt, counts, m2l_ops, boxes):
     ops, slots = src.shape
     coeffs = m2l_ops.shape[1]
-    rows = table.shape[0]
+    own, other = (g.reshape(-1, 2, coeffs // 2) for g in ghosts)
+    rows = parents.shape[0] + own.shape[0] + other.shape[0]
     chunks_per_op = slots // CHUNK
     position = jnp.arange(slots, dtype=jnp.int32)[None, :]
     tgt = jnp.where(position < counts[:, None], tgt, -1)
@@ -88,7 +297,7 @@
 
     return pl.pallas_call(
         kern,
-        in_specs=[smem, smem, vmem, anym, anym],
+        in_specs=[smem, smem, vmem, anym, anym, anym, anym],
         out_specs=vmem,
         out_shape=jax.ShapeDtypeStruct((boxes, coeffs), jnp.bfloat16),
         scratch_shapes=[
@@ -98,11 +307,11 @@
             pltpu.VMEM((2 * CHUNK, 2, 128), jnp.float32),
             pltpu.VMEM((boxes, coeffs), jnp.float32),
             pltpu.SMEM((ops * chunks_per_op + 16,), jnp.int32),
-            pltpu.SemaphoreType.DMA((2,)),
+            pltpu.SemaphoreType.DMA((4,)),
         ],
         compiler_params=pltpu.CompilerParams(vmem_limit_bytes=50 << 20),
         name="m2l",
-    )(src, nch, tgt, table, m2l_ops.reshape(ops * coeffs, coeffs))
+    )(src, nch, tgt, parents, own, other, m2l_ops.reshape(ops * coeffs, coeffs))
 
 
 def body(
@@ -120,13 +329,8 @@
     peers = boxes.shape[1]
     other = jnp.where(column == 0, boxes[2], boxes[0])
     lists = jnp.stack([boxes[1], other], 0)
-    outgoing = parents[lists]
-    mixed = lax.all_to_all(outgoing, "gy", split_axis=1, concat_axis=1, tiled=True)
-    crossed = lax.ppermute(mixed[1], "gx", [(0, 1), (1, 0)])
-    table = jnp.concatenate(
-        [parents, mixed[0].reshape(-1, coeff_count), crossed.reshape(-1, coeff_count)], 0
-    )
-    rows = table.shape[0]
+    ghosts = exchange(parents, lists)
+    rows = box_count + 2 * peers * cap
     sources = task_source[0]
     block = peers * cap
     own = jnp.logical_and(sources >= box_count, sources < box_count + block)
@@ -136,7 +340,7 @@
     src = jnp.where(sources < box_count, sources, shifted)
     src = jnp.clip(src, 0, rows - 1)
     parent_rounded = m2l(
-        table.reshape(rows, 2, 128), src, task_target[0], task_count[0], m2l_ops, box_count
+        parents.reshape(box_count, 2, -1), ghosts, src, task_target[0], task_count[0], m2l_ops, box_count
     )
     leaf_local = jnp.einsum(
         "bp,cpq->bcq", parent_rounded, l2l_ops, preferred_element_type=jnp.float32

time: 331 us -> 141 us (0.43)
  blocking collectives: 110 us -> 0 us
  local copies, waits for them, and re-layouts: 95.4 us -> 10.5 us
  Pallas kernels: 63.7 us -> 122 us
  other arithmetic: 55 us -> 2.73 us
    all_to_all x1 -> x0, blocking collectives: 110 us -> none  [body(): lax.all_to_all(outgoing, 'gy', split_axis=1, concat_axis=1, tiled=True)]
    gather x2 -> x1, local copies, waits for them, and re-layouts: 72.9 us -> 0.68 us  [exchange(): idx = jnp.transpose(lists, (1, 0, 2))[dest].reshape(-1)]
    pallas_call x1 -> x2, Pallas kernels: 63.7 us -> 122 us  [the longest x1 62.8 us: m2l(): pl.pallas_call(kern, in_specs=[smem, smem, vmem, anym, anym, anym, anym],...]
    concatenate x1 -> x0, other arithmetic: 53.9 us -> none  [body(): jnp.concatenate([parents, mixed[0].reshape(-1, coeff_count), crossed.resh...]
    concatenate x3 -> x0, local copies, waits for them, and re-layouts: 14 us -> none  [body(): jnp.concatenate([parents, mixed[0].reshape(-1, coeff_count), crossed.resh...]
    unnamed x9 -> x7, local copies, waits for them, and re-layouts: 0.07 us -> 4.93 us
    slice x1 -> x0, local copies, waits for them, and re-layouts: 3.84 us -> none  [body(): mixed[0].reshape(-1, coeff_count)]
  transfers between devices with their start and end apart: 1 -> 0, of which waited for: 0 -> 0; matrix products, arithmetic and copies ran while one was open for 2% -> 0% of each run, Pallas kernels for 0% -> 0%
where the time goes in v2:
time: 141 us; the launch traced here: 139 us
  Pallas kernels  122 us (87%)
  local copies, waits for them, and re-layouts  10.5 us (7%)
  matrix products  3.38 us (2%)
  other arithmetic  2.73 us (2%)
    pallas_call x1, Pallas kernels, m2l(): pl.pallas_call(kern, in_specs=[smem, smem, vmem, anym, anym, anym, anym],...  62.8 us
    pallas_call x1, Pallas kernels, exchange(): pl.pallas_call(comm_kernel, in_specs=[vmem, vmem], out_specs=[anym, anym]...  59.5 us
    unnamed x7, local copies, waits for them, and re-layouts  4.93 us
    dot_general x1, local copies, waits for them, and re-layouts, body(): jnp.einsum('bp,cpq->bcq', parent_rounded, l2l_ops, preferred_element_type...  4.44 us

profile of v2, /device:TPU:1, one launch (start us, length us, event | category | flops | bytes accessed | tf_op | source)
XLA Modules:
  0.0 139.0 jit_solution(8410272083182700096)
XLA Ops:
  0.0 0.0 copy-start
  0.0 0.2 stack.284
  0.2 0.7 and_select_fusion.refs_1_
  1.0 0.8 fusion.12
  1.8 0.1 add_bitcast_fusion
  1.9 0.7 gather_fusion
  2.5 1.0 copy.18
  3.5 0.1 fusion.10
  3.7 1.0 bitcast_select_fusion
  4.7 2.7 %fusion.5 = bf16[512,256]{0,1:T(8,128)(2,1)S(1)} fusion(bf16[8,256,256]{2,1,0:T(8,128)(2,1)} %param.9, bf16[512,8,256]{2,1,0:T(8,128)(2,1)} %bitcast.104), kind=kOutput, calls=%fused_computation.5 | convolution fusion | flops 537001984 | bytes 3407872 | tf_op jit(solution)/shard_map/bcp,cpq->bq/dot_general | solution.py:324
  7.4 0.2 copy.17.own_block.refs_3_
  7.6 59.5 %exchange.1 = (bf16[64,128,2,128]{3,2,1,0:T(2,128)(2,1)S(1)}, bf16[64,128,2,128]{3,2,1,0:T(2,128)(2,1)S(1)}) custom-call(s32[21504]{0:T(1024)S(1)} %bitcast.96, bf16[512,2,128]{2,1,0:T(2,128)(2,1)S(1)} %copy.17.own_block.refs_3_), custom_call_target="tpu_custom_call" | custom-call | tf_op jit(solution)/shard_map/exchange/pallas_call | solution.py:188
  67.1 0.0 copy-start.1
  67.1 2.0 %copy-done.1 = bf16[64,128,2,128]{3,2,1,0:T(2,128)(2,1)} copy-done((bf16[64,128,2,128]{3,2,1,0:T(2,128)(2,1)}, bf16[64,128,2,128]{3,2,1,0:T(2,128)(2,1)S(1)}, u32[]{:S(2)}) %copy-start.1) | copy-done | bytes 4194328
  69.1 0.0 copy-start.2
  69.1 1.9 %copy-done.2 = bf16[64,128,2,128]{3,2,1,0:T(2,128)(2,1)} copy-done((bf16[64,128,2,128]{3,2,1,0:T(2,128)(2,1)}, bf16[64,128,2,128]{3,2,1,0:T(2,128)(2,1)S(1)}, u32[]{:S(2)}) %copy-start.2) | copy-done | bytes 4194328
  71.1 62.8 %m2l.1 = bf16[512,256]{1,0:T(8,128)(2,1)S(1)} custom-call(s32[49664]{0:T(1024)S(1)} %concatenate.25.refs_0_, s32[96]{0:T(128)S(1)} %and_select_fusion.refs_1_, s32[416,128]{1,0:T(8,128)S(1)} %reshape.3253.refs_2_, bf16[512,2,128]{2,1,0:T(2,128)(2,1)S(1)} %copy.17.own_block.refs_3_, bf16[8192,2,128]{2,1,0:T(2,128)(2,1)} %bitcast.94, ...), custom_call_target="tpu_custom_call" | custom-call | tf_op jit(solution)/shard_map/m2l/pallas_call | solution.py:298
  133.9 0.0 copy-done
  133.9 0.7 fusion.8
  134.6 4.4 %copy.26 = f32[512,8,256]{2,1,0:T(8,128)} copy(f32[512,8,256]{2,0,1:T(8,128)S(1)} %fusion.8) | data formatting | bytes 8388608 | tf_op jit(solution)/shard_map/bp,cpq->bcq/dot_general | solution.py:345
  (5 shorter events, 0.1 us)
Async XLA Ops:
  0.0 133.9 %copy-start = (bf16[8,256,256]{2,1,0:T(8,128)(2,1)S(1)}, bf16[8,256,256]{2,1,0:T(8,128)(2,1)}, u32[]{:S(2)}) copy-start(bf16[8,256,256]{2,1,0:T(8,128)(2,1)} %param.11) | copy-start | bytes 3145732
  67.1 2.0 %copy-start.1 = (bf16[64,128,2,128]{3,2,1,0:T(2,128)(2,1)}, bf16[64,128,2,128]{3,2,1,0:T(2,128)(2,1)S(1)}, u32[]{:S(2)}) copy-start(bf16[64,128,2,128]{3,2,1,0:T(2,128)(2,1)S(1)} %get-tuple-element.7) | copy-start | bytes 12582916
  69.1 1.9 %copy-start.2 = (bf16[64,128,2,128]{3,2,1,0:T(2,128)(2,1)}, bf16[64,128,2,128]{3,2,1,0:T(2,128)(2,1)S(1)}, u32[]{:S(2)}) copy-start(bf16[64,128,2,128]{3,2,1,0:T(2,128)(2,1)S(1)} %get-tuple-element.8) | copy-start | bytes 12582916

commit v3 on v2

--- a/solution.py
+++ b/solution.py
@@ -6,6 +6,7 @@
 from jax.sharding import PartitionSpec as P
 
 CHUNK = 128
+BATCH = 4
 SIDE = 4
 UNROLL = 16
 
@@ -56,15 +57,15 @@
     return parts[0] + parts[1] + parts[2]
 
 
-def comm_kernel(idx_in, own_block, ghost_own, ghost_other, *scratch):
+def comm_kernel(peers, idx_in, own_block, table, *scratch):
     blocks = dict(zip(INTERNAL, (own_block,) + scratch[: len(INTERNAL) - 1]))
     scratch = scratch[len(INTERNAL) - 1 :]
     (land, idx, stage_own, stage_other, full_send, full_recv, idx_send, idx_recv, idx_load,
-     own_send, own_recv, own_local, other_send, other_recv) = scratch
+     own_send, own_recv, own_local, other_send, other_recv, self_local) = scratch
     groups, order, pos = list_layout()
     slot = {o: i for i, o in enumerate(INTERNAL)}
-    peers = ghost_own.shape[0]
-    cap = ghost_own.shape[1]
+    cap = stage_own.shape[1]
+    boxes = own_block.shape[0]
     half_rows = own_block.shape[0] // 2
     pair = 2 * cap
     me_u = lax.axis_index("gx")
@@ -83,6 +84,10 @@
                             device_id_type=pl.DeviceIdType.MESH)
     pl.semaphore_wait(ready, len(sends))
 
+    def ghost(side, owner, count=1):
+        first = boxes + (side * peers + owner) * cap
+        return table.at[pl.ds(first, count * cap)]
+
     def remote(src, dst, send, recv, target):
         return pltpu.make_async_remote_copy(
             src_ref=src, dst_ref=dst, send_sem=send, recv_sem=recv, device_id=target,
@@ -109,6 +114,8 @@
         src = idx_in if o == 0 else land
         return pltpu.make_async_copy(src.at[part], idx.at[part], idx_load.at[slot[o]])
 
+    self_copy = pltpu.make_async_copy(own_block, table.at[pl.ds(0, boxes)], self_local)
+    self_copy.start()
     children = {o: [c for c in INTERNAL if PARENT[c] == o] for o in INTERNAL}
     loaded = set()
     for kind, o, arg in PLAN:
@@ -145,21 +152,23 @@
         owner = torus_add(me_v, o, -1)
         step = torus_step(o, arg) if arg != o else 0
         if arg == o:
-            pltpu.make_async_copy(stage_own.at[p], ghost_own.at[owner], own_local).start()
+            pltpu.make_async_copy(stage_own.at[p], ghost(0, owner), own_local).start()
         else:
-            remote(stage_own.at[p], ghost_own.at[owner], own_send, own_recv, mesh_id(step)).start()
-        remote(stage_other.at[p], ghost_other.at[owner], other_send, other_recv,
+            remote(stage_own.at[p], ghost(0, owner), own_send, own_recv, mesh_id(step)).start()
+        remote(stage_other.at[p], ghost(1, owner), other_send, other_recv,
                mesh_id(step, 1)).start()
 
     here = (1 - me_u, me_v)
     inner = len(INTERNAL)
-    part = ghost_own.at[pl.ds(0, peers - inner)]
+    part = ghost(0, 0, peers - inner)
+    side = ghost(1, 0, peers)
     remote(part, part, own_send, own_recv, here).wait_recv()
-    remote(ghost_other, ghost_other, other_send, other_recv, here).wait_recv()
+    remote(side, side, other_send, other_recv, here).wait_recv()
     remote(part, part, own_send, own_recv, here).wait_send()
-    remote(ghost_other, ghost_other, other_send, other_recv, here).wait_send()
-    part = ghost_own.at[pl.ds(0, inner)]
+    remote(side, side, other_send, other_recv, here).wait_send()
+    part = ghost(0, 0, inner)
     pltpu.make_async_copy(part, part, own_local).wait()
+    self_copy.wait()
     for c in INTERNAL[1:]:
         idx_copy(c).wait_send()
         for half in range(2):
@@ -182,14 +191,16 @@
     idx = jnp.transpose(lists, (1, 0, 2))[dest].reshape(-1)
     inner = len(INTERNAL)
     dma = pltpu.SemaphoreType.DMA
-    anym = pl.BlockSpec(memory_space=pl.ANY)
     vmem = pl.BlockSpec(memory_space=pltpu.VMEM)
-    ghost = jax.ShapeDtypeStruct((peers, cap, 2, coeffs // 2), parents.dtype)
+
+    def kern(*refs):
+        comm_kernel(peers, *refs)
+
     return pl.pallas_call(
-        comm_kernel,
+        kern,
         in_specs=[vmem, vmem],
-        out_specs=[anym, anym],
-        out_shape=[ghost, ghost],
+        out_specs=vmem,
+        out_shape=pltpu.VMEM((boxes + 2 * peers * cap, 2, coeffs // 2), parents.dtype),
         scratch_shapes=[pltpu.VMEM((boxes, 2, coeffs // 2), parents.dtype)] * (inner - 1)
         + [
             pltpu.VMEM(idx.shape, jnp.int32),
@@ -201,29 +212,22 @@
             dma((inner - 1,)),
             dma((inner - 1,)),
             dma((inner,)),
-            dma, dma, dma, dma, dma,
+            dma, dma, dma, dma, dma, dma,
         ],
         compiler_params=pltpu.CompilerParams(
-            collective_id=0, has_side_effects=True, vmem_limit_bytes=40 << 20
+            collective_id=0, has_side_effects=True, vmem_limit_bytes=20 << 20
         ),
         name="exchange",
     )(idx, parents.reshape(boxes, 2, coeffs // 2))
 
 
-def m2l_kernel(ops, chunks_per_op, src_ref, nch_ref, tgt_ref, par_hbm, own_hbm, other_hbm, op_hbm, out_ref,
-               tab_ref, op_ref, xa_ref, xb_ref, acc_ref, list_ref, sem):
-    coeffs = acc_ref.shape[1]
-    boxes = acc_ref.shape[0]
-    loads = []
-    first = 0
-    for i, part in enumerate((par_hbm, own_hbm, other_hbm)):
-        n = part.shape[0]
-        loads.append(pltpu.make_async_copy(part, tab_ref.at[pl.ds(first, n)], sem.at[1 + i]))
-        loads[-1].start()
-        first += n
-    load_ops = pltpu.make_async_copy(op_hbm, op_ref, sem.at[0])
-    load_ops.start()
+def m2l_kernel(ops, chunks_per_op, src_ref, nch_ref, tgt_ref, tab_ref, op_ref, out_ref,
+               x_ref, y_ref, acc_ref, list_ref):
+    boxes, coeffs = acc_ref.shape
+    stride = src_ref.shape[0] // CHUNK
+    empty = ops * chunks_per_op
     acc_ref[...] = jnp.zeros_like(acc_ref)
+    y_ref[...] = jnp.zeros_like(y_ref)
 
     def fill(o, pos):
         n = nch_ref[o]
@@ -232,86 +236,88 @@
             pos = pos + jnp.where(c < n, 1, 0)
         return pos
 
-    total = lax.fori_loop(0, ops, fill, 0)
-    for i in range(8):
-        list_ref[total + i] = ops * chunks_per_op
-    for load in loads:
-        load.wait()
-    load_ops.wait()
-
-    def gather(it, x_ref):
-        for h in range(2):
-            b = list_ref[2 * it + h] * CHUNK
+    for i in range(BATCH):
+        list_ref[i] = empty
+    total = lax.fori_loop(0, ops, fill, BATCH)
+    for i in range(3 * BATCH):
+        list_ref[total + i] = empty
+
+    def gather(it):
+        for h in range(BATCH):
+            ch = list_ref[BATCH * it + h]
             for i in range(CHUNK):
-                x_ref[h * CHUNK + i] = tab_ref[src_ref[b + i]].astype(jnp.float32)
-
-    def compute(it, x_ref):
-        x2 = x_ref.reshape(4 * CHUNK, 128)
-        ys, ps = [], []
-        rows = lax.broadcasted_iota(jnp.int32, (boxes, CHUNK), 0)
-        for h in range(2):
-            ch = list_ref[2 * it + h]
-            lo = x2[pl.ds(h * 2 * CHUNK, CHUNK, stride=2), :].astype(jnp.bfloat16)
-            hi = x2[pl.ds(h * 2 * CHUNK + 1, CHUNK, stride=2), :].astype(jnp.bfloat16)
-            xx = jnp.concatenate([lo, hi], axis=1)
+                s = src_ref.at[pl.ds(i * stride, stride)][ch]
+                x_ref[h * CHUNK + i] = tab_ref[s].astype(jnp.float32)
+
+    def translate(it):
+        x2 = x_ref.reshape(2 * BATCH * CHUNK, x_ref.shape[2])
+        for h in range(BATCH):
+            ch = list_ref[BATCH * it + h]
+            first = 2 * CHUNK * h
+            lo = x2[pl.ds(first, CHUNK, stride=2), :].astype(jnp.bfloat16)
+            hi = x2[pl.ds(first + 1, CHUNK, stride=2), :].astype(jnp.bfloat16)
             o = jnp.minimum(lax.div(ch, chunks_per_op), ops - 1)
             w = op_ref[pl.ds(pl.multiple_of(o * coeffs, coeffs), coeffs), :]
-            ys.append(jnp.dot(xx, w, preferred_element_type=jnp.float32).astype(jnp.bfloat16))
-            t = tgt_ref[pl.ds(ch, 1), :]
+            y_ref[h * CHUNK : (h + 1) * CHUNK, :] = jnp.dot(
+                jnp.concatenate([lo, hi], axis=1), w, preferred_element_type=jnp.float32
+            ).astype(jnp.bfloat16)
+
+    def scatter(it):
+        rows = lax.broadcasted_iota(jnp.int32, (boxes, CHUNK), 0)
+        ps = []
+        for h in range(BATCH):
+            t = tgt_ref[pl.ds(list_ref[BATCH * it + h], 1), :]
             ps.append(jnp.where(rows == t, 1.0, 0.0).astype(jnp.bfloat16))
         acc_ref[...] += jnp.dot(
-            jnp.concatenate(ps, axis=1), jnp.concatenate(ys, axis=0),
-            preferred_element_type=jnp.float32,
+            jnp.concatenate(ps, axis=1), y_ref[...], preferred_element_type=jnp.float32
         )
 
-    gather(0, xa_ref)
-
-    @pl.loop(0, lax.div(total + 3, 4))
+    gather(1)
+
+    @pl.loop(1, lax.div(total + BATCH - 1, BATCH) + 1)
     def _(j):
-        gather(2 * j + 1, xb_ref)
-        compute(2 * j, xa_ref)
-        gather(2 * j + 2, xa_ref)
-        compute(2 * j + 1, xb_ref)
+        scatter(j - 1)
+        translate(j)
+        gather(j + 1)
 
     out_ref[...] = acc_ref[...].astype(out_ref.dtype)
 
 
-def m2l(parents, ghosts, src, tgt, counts, m2l_ops, boxes):
+def m2l(table, src, tgt, counts, m2l_ops, boxes):
     ops, slots = src.shape
     coeffs = m2l_ops.shape[1]
-    own, other = (g.reshape(-1, 2, coeffs // 2) for g in ghosts)
-    rows = parents.shape[0] + own.shape[0] + other.shape[0]
     chunks_per_op = slots // CHUNK
+    chunks = ops * chunks_per_op
     position = jnp.arange(slots, dtype=jnp.int32)[None, :]
     tgt = jnp.where(position < counts[:, None], tgt, -1)
-    tgt = jnp.concatenate([tgt, jnp.full((8, slots), -1, jnp.int32)], 0)
-    tgt = tgt.reshape(-1, CHUNK)
-    src = jnp.concatenate([src.reshape(-1), jnp.zeros((slots,), jnp.int32)], 0)
+    tgt = jnp.pad(tgt.reshape(-1, CHUNK), ((0, 8), (0, 0)), constant_values=-1)
+    stride = -(-(chunks + 1) // 128) * 128
+    src = jnp.pad(src.reshape(-1, CHUNK).T, ((0, 0), (0, stride - chunks))).reshape(-1)
     nch = (counts + (CHUNK - 1)) // CHUNK
     smem = pl.BlockSpec(memory_space=pltpu.SMEM)
     vmem = pl.BlockSpec(memory_space=pltpu.VMEM)
-    anym = pl.BlockSpec(memory_space=pl.ANY)
 
     def kern(*refs):
         m2l_kernel(ops, chunks_per_op, *refs)
 
     return pl.pallas_call(
         kern,
-        in_specs=[smem, smem, vmem, anym, anym, anym, anym],
+        in_specs=[smem, smem, vmem, vmem, vmem],
         out_specs=vmem,
         out_shape=jax.ShapeDtypeStruct((boxes, coeffs), jnp.bfloat16),
         scratch_shapes=[
-            pltpu.VMEM((rows, 2, 128), jnp.bfloat16),
-            pltpu.VMEM((ops * coeffs, coeffs), jnp.bfloat16),
-            pltpu.VMEM((2 * CHUNK, 2, 128), jnp.float32),
-            pltpu.VMEM((2 * CHUNK, 2, 128), jnp.float32),
+            pltpu.VMEM((BATCH * CHUNK, 2, coeffs // 2), jnp.float32),
+            pltpu.VMEM((BATCH * CHUNK, coeffs), jnp.bfloat16),
             pltpu.VMEM((boxes, coeffs), jnp.float32),
-            pltpu.SMEM((ops * chunks_per_op + 16,), jnp.int32),
-            pltpu.SemaphoreType.DMA((4,)),
+            pltpu.SMEM((chunks + 4 * BATCH,), jnp.int32),
         ],
-        compiler_params=pltpu.CompilerParams(vmem_limit_bytes=50 << 20),
+        compiler_params=pltpu.CompilerParams(vmem_limit_bytes=8 << 20),
         name="m2l",
-    )(src, nch, tgt, parents, own, other, m2l_ops.reshape(ops * coeffs, coeffs))
+    )(
+        src, nch, tgt,
+        pltpu.with_memory_space_constraint(table, pltpu.VMEM),
+        pltpu.with_memory_space_constraint(m2l_ops.reshape(ops * coeffs, coeffs), pltpu.VMEM),
+    )
 
 
 def body(
@@ -329,8 +335,8 @@
     peers = boxes.shape[1]
     other = jnp.where(column == 0, boxes[2], boxes[0])
     lists = jnp.stack([boxes[1], other], 0)
-    ghosts = exchange(parents, lists)
-    rows = box_count + 2 * peers * cap
+    table = exchange(parents, lists)
+    rows = table.shape[0]
     sources = task_source[0]
     block = peers * cap
     own = jnp.logical_and(sources >= box_count, sources < box_count + block)
@@ -340,7 +346,7 @@
     src = jnp.where(sources < box_count, sources, shifted)
     src = jnp.clip(src, 0, rows - 1)
     parent_rounded = m2l(
-        parents.reshape(box_count, 2, -1), ghosts, src, task_target[0], task_count[0], m2l_ops, box_count
+        table, src, task_target[0], task_count[0], m2l_ops, box_count
     )
     leaf_local = jnp.einsum(
         "bp,cpq->bcq", parent_rounded, l2l_ops, preferred_element_type=jnp.float32

time: 141 us -> 117 us (0.83)
  Pallas kernels: 122 us -> 93.8 us
  local copies, waits for them, and re-layouts: 10.5 us -> 17.4 us
  other arithmetic: 2.73 us -> 1.17 us
    pallas_call x2, Pallas kernels: 122 us -> 93.8 us  [the longest x1 59.6 us: exchange(): pl.pallas_call(kern, in_specs=[vmem, vmem], out_specs=vmem, out_shape=plt...]
    unnamed x7 -> x16, local copies, waits for them, and re-layouts: 4.93 us -> 11.5 us
where the time goes in v3:
time: 117 us; the launch traced here: 116 us
  Pallas kernels  93.8 us (80%)
  local copies, waits for them, and re-layouts  17.4 us (15%)
  matrix products  3.38 us (3%)
  other arithmetic  1.17 us (1%)
    pallas_call x1, Pallas kernels, exchange(): pl.pallas_call(kern, in_specs=[vmem, vmem], out_specs=vmem, out_shape=plt...  59.6 us
    pallas_call x1, Pallas kernels, m2l(): pl.pallas_call(kern, in_specs=[smem, smem, vmem, vmem, vmem], out_specs=v...  34.2 us
    unnamed x16, local copies, waits for them, and re-layouts  11.5 us
    dot_general x1, local copies, waits for them, and re-layouts, body(): jnp.einsum('bp,cpq->bcq', parent_rounded, l2l_ops, preferred_element_type...  4.44 us
    dot_general x1, matrix products, body(): jnp.einsum('bcp,cpq->bq', leaves, m2m_ops, preferred_element_type=jnp.flo...  2.67 us

profile of v3, /device:TPU:1, one launch (start us, length us, event | category | flops | bytes accessed | tf_op | source)
XLA Modules:
  0.0 115.9 jit_solution(13249877812554350580)
XLA Ops:
  0.0 0.0 copy-start
  0.0 0.2 stack.284
  0.3 0.9 fusion.13
  1.1 0.1 add_bitcast_fusion
  1.2 0.7 gather_fusion
  1.9 2.7 %fusion.5 = bf16[512,256]{0,1:T(8,128)(2,1)S(1)} fusion(bf16[8,256,256]{2,1,0:T(8,128)(2,1)} %param.9, bf16[512,8,256]{2,1,0:T(8,128)(2,1)} %bitcast.102), kind=kOutput, calls=%fused_computation.5 | convolution fusion | flops 537001984 | bytes 3407872 | tf_op jit(solution)/shard_map/bcp,cpq->bq/dot_general | solution.py:330
  4.5 0.2 copy.23.refs_1_
  4.7 0.0 copy-start.4
  4.7 0.0 copy-start.5
  4.7 0.0 copy-start.6
  4.7 59.6 %exchange.1.refs_3_ = bf16[16896,2,128]{2,1,0:T(2,128)(2,1)S(1)} custom-call(s32[21504]{0:T(1024)S(1)} %bitcast.96, bf16[512,2,128]{2,1,0:T(2,128)(2,1)S(1)} %copy.23.refs_1_), custom_call_target="tpu_custom_call" | custom-call | tf_op jit(solution)/shard_map/exchange/pallas_call | solution.py:199
  64.4 3.3 %copy-done.1 = bf16[16896,2,128]{2,1,0:T(2,128)(2,1)} copy-done((bf16[16896,2,128]{2,1,0:T(2,128)(2,1)}, bf16[16896,2,128]{2,1,0:T(2,128)(2,1)S(1)}, u32[]{:S(2)}) %copy-start.1) | copy-done | bytes 8650776
  67.7 0.1 copy.12
  67.9 0.1 fusion.11
  68.0 0.1 copy.24
  68.2 0.0 copy-done.6
  68.2 0.1 lt.58
  68.2 0.1 lt.59
  68.4 0.1 compare_select_fusion.1
  68.5 3.4 %copy-done.2 = bf16[16896,2,128]{2,1,0:T(2,128)(2,1)S(1)} copy-done((bf16[16896,2,128]{2,1,0:T(2,128)(2,1)S(1)}, bf16[16896,2,128]{2,1,0:T(2,128)(2,1)}, u32[]{:S(2)}) %copy-start.2) | copy-done | bytes 8650776
  72.0 4.6 %copy-done.3 = bf16[96,256,256]{2,1,0:T(8,128)(2,1)S(1)} copy-done((bf16[96,256,256]{2,1,0:T(8,128)(2,1)S(1)}, bf16[96,256,256]{2,1,0:T(8,128)(2,1)}, u32[]{:S(2)}) %copy-start.3) | copy-done | bytes 12582936
  76.6 34.2 %m2l.1 = bf16[512,256]{1,0:T(8,128)(2,1)S(1)} custom-call(s32[65536]{0:T(1024)S(1)} %bitcast.95, s32[96]{0:T(128)S(1)} %and_select_fusion.refs_1_, s32[392,128]{1,0:T(8,128)S(1)} %pad.9.refs_2_, bf16[16896,2,128]{2,1,0:T(2,128)(2,1)S(1)} %copy-done.2, bf16[24576,256]{1,0:T(8,128)(2,1)S(1)} %bitcast.94), custom_call_target="tpu_custom_call" | custom-call | tf_op jit(solution)/shard_map/m2l/pallas_call | solution.py:303
  110.8 0.7 fusion.8
  111.5 4.4 %copy.32 = f32[512,8,256]{2,1,0:T(8,128)} copy(f32[512,8,256]{2,0,1:T(8,128)S(1)} %fusion.8) | data formatting | bytes 8388608 | tf_op jit(solution)/shard_map/bp,cpq->bcq/dot_general | solution.py:351
  (15 shorter events, 0.1 us)
Async XLA Ops:
  0.0 110.8 %copy-start = (bf16[8,256,256]{2,1,0:T(8,128)(2,1)S(1)}, bf16[8,256,256]{2,1,0:T(8,128)(2,1)}, u32[]{:S(2)}) copy-start(bf16[8,256,256]{2,1,0:T(8,128)(2,1)} %param.11) | copy-start | bytes 3145732
  4.7 63.0 %copy-start.4 = (s32[1,96,512]{2,1,0:T(8,128)S(1)}, s32[1,96,512]{2,1,0:T(8,128)}, u32[]{:S(2)}) copy-start(s32[1,96,512]{2,1,0:T(8,128)} %param.13) | copy-start | bytes 589828
  4.7 63.4 %copy-start.5 = (s32[1,96,512]{2,1,0:T(8,128)S(1)}, s32[1,96,512]{2,1,0:T(8,128)}, u32[]{:S(2)}) copy-start(s32[1,96,512]{2,1,0:T(8,128)} %param.14) | copy-start | bytes 589828
  4.7 63.4 %copy-start.6 = (s32[1,96]{1,0:T(1,128)S(1)}, s32[1,96]{1,0:T(1,128)}, u32[]{:S(2)}) copy-start(s32[1,96]{1,0:T(1,128)} %param.15) | copy-start | bytes 1156
  64.4 3.3 %copy-start.1 = (bf16[16896,2,128]{2,1,0:T(2,128)(2,1)}, bf16[16896,2,128]{2,1,0:T(2,128)(2,1)S(1)}, u32[]{:S(2)}) copy-start(bf16[16896,2,128]{2,1,0:T(2,128)(2,1)S(1)} %exchange.1.refs_3_) | copy-start | bytes 25952260
  68.5 3.5 %copy-start.2 = (bf16[16896,2,128]{2,1,0:T(2,128)(2,1)S(1)}, bf16[16896,2,128]{2,1,0:T(2,128)(2,1)}, u32[]{:S(2)}) copy-start(bf16[16896,2,128]{2,1,0:T(2,128)(2,1)} %copy-done.1) | copy-start | bytes 25952260
  72.0 4.6 %copy-start.3 = (bf16[96,256,256]{2,1,0:T(8,128)(2,1)S(1)}, bf16[96,256,256]{2,1,0:T(8,128)(2,1)}, u32[]{:S(2)}) copy-start(bf16[96,256,256]{2,1,0:T(8,128)(2,1)} %param.10) | copy-start | bytes 37748740

commit v4 on v3

--- a/solution.py
+++ b/solution.py
@@ -8,7 +8,7 @@
 CHUNK = 128
 BATCH = 4
 SIDE = 4
-UNROLL = 16
+UNROLL = 32
 
 INTERNAL = (0, 12, 4, 48, 28, 7, 49, 52, 29, 11, 6, 23, 45, 10, 22, 41, 46, 47)
 PARENT = (-1, 0, 6, 7, 0, 6, 7, 4, 12, 10, 6, 7, 0, 29, 10, 12, 0, 29, 22, 23, 4, 22, 23, 7, 28, 41, 22, 11, 12, 28, 29, 47, 48, 49, 46, 47, 52, 41, 22, 23, 41, 45, 41, 47, 45, 29, 45, 46, 0, 48, 49, 48, 48, 52, 6, 7, 52, 41, 10, 11, 12, 49, 46, 47)
@@ -57,11 +57,11 @@
     return parts[0] + parts[1] + parts[2]
 
 
-def comm_kernel(peers, idx_in, own_block, table, *scratch):
+def comm_kernel(peers, idx_in, own_block, ops_in, src_in, tgt_in, table, ops_out, src_out, tgt_out, *scratch):
     blocks = dict(zip(INTERNAL, (own_block,) + scratch[: len(INTERNAL) - 1]))
     scratch = scratch[len(INTERNAL) - 1 :]
     (land, idx, stage_own, stage_other, full_send, full_recv, idx_send, idx_recv, idx_load,
-     own_send, own_recv, own_local, other_send, other_recv, self_local) = scratch
+     own_send, own_recv, own_local, other_send, other_recv, keep) = scratch
     groups, order, pos = list_layout()
     slot = {o: i for i, o in enumerate(INTERNAL)}
     cap = stage_own.shape[1]
@@ -114,8 +114,11 @@
         src = idx_in if o == 0 else land
         return pltpu.make_async_copy(src.at[part], idx.at[part], idx_load.at[slot[o]])
 
-    self_copy = pltpu.make_async_copy(own_block, table.at[pl.ds(0, boxes)], self_local)
-    self_copy.start()
+    kept = [(own_block, table.at[pl.ds(0, boxes)]), (ops_in, ops_out), (src_in, src_out),
+            (tgt_in, tgt_out)]
+    kept = [pltpu.make_async_copy(a, b, keep.at[i]) for i, (a, b) in enumerate(kept)]
+    for copy in kept:
+        copy.start()
     children = {o: [c for c in INTERNAL if PARENT[c] == o] for o in INTERNAL}
     loaded = set()
     for kind, o, arg in PLAN:
@@ -139,16 +142,15 @@
             loaded.add(o)
         block = blocks[o]
         p = pos[arg]
-        for h, stage in ((0, stage_own), (1, stage_other)):
-
-            def pick(g, carry, block=block, stage=stage, h=h, p=p):
-                b = p * pair + h * cap + g * UNROLL
-                rows = [block[idx[b + i]] for i in range(UNROLL)]
+
+        def pick(g, carry, block=block, p=p):
+            for h, stage in ((0, stage_own), (1, stage_other)):
                 for i in range(UNROLL):
-                    stage[p, g * UNROLL + i] = rows[i]
-                return carry
-
-            lax.fori_loop(0, cap // UNROLL, pick, 0)
+                    row = block[idx.at[pl.ds(p * pair + h * cap + i, cap)][g * UNROLL]]
+                    stage[p, g * UNROLL + i] = row
+            return carry
+
+        lax.fori_loop(0, cap // UNROLL, pick, 0)
         owner = torus_add(me_v, o, -1)
         step = torus_step(o, arg) if arg != o else 0
         if arg == o:
@@ -168,7 +170,8 @@
     remote(side, side, other_send, other_recv, here).wait_send()
     part = ghost(0, 0, inner)
     pltpu.make_async_copy(part, part, own_local).wait()
-    self_copy.wait()
+    for copy in kept:
+        copy.wait()
     for c in INTERNAL[1:]:
         idx_copy(c).wait_send()
         for half in range(2):
@@ -182,7 +185,7 @@
     return step
 
 
-def exchange(parents, lists):
+def exchange(parents, lists, ops, src, tgt):
     _, peers, cap = lists.shape
     boxes, coeffs = parents.shape
     groups, order, pos = list_layout()
@@ -192,19 +195,25 @@
     inner = len(INTERNAL)
     dma = pltpu.SemaphoreType.DMA
     vmem = pl.BlockSpec(memory_space=pltpu.VMEM)
+    anym = pl.BlockSpec(memory_space=pl.ANY)
 
     def kern(*refs):
         comm_kernel(peers, *refs)
 
     return pl.pallas_call(
         kern,
-        in_specs=[vmem, vmem],
-        out_specs=vmem,
-        out_shape=pltpu.VMEM((boxes + 2 * peers * cap, 2, coeffs // 2), parents.dtype),
+        in_specs=[vmem, vmem, anym, anym, anym],
+        out_specs=[vmem] * 4,
+        out_shape=[
+            pltpu.VMEM((boxes + 2 * peers * cap, 2, coeffs // 2), parents.dtype),
+            pltpu.VMEM(ops.shape, ops.dtype),
+            pltpu.VMEM(src.shape, src.dtype),
+            pltpu.VMEM(tgt.shape, tgt.dtype),
+        ],
         scratch_shapes=[pltpu.VMEM((boxes, 2, coeffs // 2), parents.dtype)] * (inner - 1)
         + [
             pltpu.VMEM(idx.shape, jnp.int32),
-            pltpu.SMEM(idx.shape, jnp.int32),
+            pltpu.SMEM((idx.shape[0] + 1024,), jnp.int32),
             pltpu.VMEM((len(order), cap, 2, coeffs // 2), parents.dtype),
             pltpu.VMEM((len(order), cap, 2, coeffs // 2), parents.dtype),
             dma((2 * inner - 2,)),
@@ -212,16 +221,17 @@
             dma((inner - 1,)),
             dma((inner - 1,)),
             dma((inner,)),
-            dma, dma, dma, dma, dma, dma,
+            dma, dma, dma, dma, dma,
+            dma((4,)),
         ],
         compiler_params=pltpu.CompilerParams(
             collective_id=0, has_side_effects=True, vmem_limit_bytes=20 << 20
         ),
         name="exchange",
-    )(idx, parents.reshape(boxes, 2, coeffs // 2))
-
-
-def m2l_kernel(ops, chunks_per_op, src_ref, nch_ref, tgt_ref, tab_ref, op_ref, out_ref,
+    )(idx, parents.reshape(boxes, 2, coeffs // 2), ops, src, tgt)
+
+
+def m2l_kernel(ops, chunks_per_op, src_ref, count_ref, tgt_ref, tab_ref, op_ref, out_ref,
                x_ref, y_ref, acc_ref, list_ref):
     boxes, coeffs = acc_ref.shape
     stride = src_ref.shape[0] // CHUNK
@@ -230,7 +240,7 @@
     y_ref[...] = jnp.zeros_like(y_ref)
 
     def fill(o, pos):
-        n = nch_ref[o]
+        n = lax.div(count_ref[o] + (CHUNK - 1), CHUNK)
         for c in range(chunks_per_op):
             list_ref[pos] = o * chunks_per_op + c
             pos = pos + jnp.where(c < n, 1, 0)
@@ -283,17 +293,22 @@
     out_ref[...] = acc_ref[...].astype(out_ref.dtype)
 
 
-def m2l(table, src, tgt, counts, m2l_ops, boxes):
+def prepare(src, tgt, counts):
     ops, slots = src.shape
-    coeffs = m2l_ops.shape[1]
-    chunks_per_op = slots // CHUNK
-    chunks = ops * chunks_per_op
+    chunks = ops * slots // CHUNK
     position = jnp.arange(slots, dtype=jnp.int32)[None, :]
     tgt = jnp.where(position < counts[:, None], tgt, -1)
     tgt = jnp.pad(tgt.reshape(-1, CHUNK), ((0, 8), (0, 0)), constant_values=-1)
     stride = -(-(chunks + 1) // 128) * 128
     src = jnp.pad(src.reshape(-1, CHUNK).T, ((0, 0), (0, stride - chunks))).reshape(-1)
-    nch = (counts + (CHUNK - 1)) // CHUNK
+    return src, tgt
+
+
+def m2l(table, src, tgt, counts, m2l_ops, slots, boxes):
+    ops = counts.shape[0]
+    coeffs = m2l_ops.shape[1]
+    chunks_per_op = slots // CHUNK
+    chunks = ops * chunks_per_op
     smem = pl.BlockSpec(memory_space=pltpu.SMEM)
     vmem = pl.BlockSpec(memory_space=pltpu.VMEM)
 
@@ -314,9 +329,11 @@
         compiler_params=pltpu.CompilerParams(vmem_limit_bytes=8 << 20),
         name="m2l",
     )(
-        src, nch, tgt,
+        src,
+        counts,
+        pltpu.with_memory_space_constraint(tgt, pltpu.VMEM),
         pltpu.with_memory_space_constraint(table, pltpu.VMEM),
-        pltpu.with_memory_space_constraint(m2l_ops.reshape(ops * coeffs, coeffs), pltpu.VMEM),
+        pltpu.with_memory_space_constraint(m2l_ops, pltpu.VMEM),
     )
 
 
@@ -335,19 +352,20 @@
     peers = boxes.shape[1]
     other = jnp.where(column == 0, boxes[2], boxes[0])
     lists = jnp.stack([boxes[1], other], 0)
-    table = exchange(parents, lists)
-    rows = table.shape[0]
     sources = task_source[0]
     block = peers * cap
+    rows = box_count + 2 * block
     own = jnp.logical_and(sources >= box_count, sources < box_count + block)
     shifted = jnp.where(
         jnp.logical_and(column == 1, own), sources + block, sources - block
     )
     src = jnp.where(sources < box_count, sources, shifted)
     src = jnp.clip(src, 0, rows - 1)
-    parent_rounded = m2l(
-        table, src, task_target[0], task_count[0], m2l_ops, box_count
-    )
+    src, tgt = prepare(src, task_target[0], task_count[0])
+    ops = m2l_ops.reshape(-1, coeff_count)
+    table, ops, src, tgt = exchange(parents, lists, ops, src, tgt)
+    slots = task_target.shape[2]
+    parent_rounded = m2l(table, src, tgt, task_count[0], ops, slots, box_count)
     leaf_local = jnp.einsum(
         "bp,cpq->bcq", parent_rounded, l2l_ops, preferred_element_type=jnp.float32
     )

time: 117 us -> 112 us (0.957)
  local copies, waits for them, and re-layouts: 17.4 us -> 13.2 us
    unnamed x16 -> x10, local copies, waits for them, and re-layouts: 11.5 us -> 4.67 us
    pallas_call x1, Pallas kernels: 34.2 us -> 36.5 us  [m2l(): pl.pallas_call(kern, in_specs=[smem, smem, vmem, vmem, vmem], out_specs=v...]
    pallas_call x1, Pallas kernels: 59.6 us -> 58 us  [exchange(): pl.pallas_call(kern, in_specs=[vmem, vmem, anym, anym, anym], out_specs=[...]
where the time goes in v4:
time: 112 us
  Pallas kernels  94.5 us (84%)
  local copies, waits for them, and re-layouts  13.2 us (12%)
  matrix products  3.11 us (3%)
    pallas_call x1, Pallas kernels, exchange(): pl.pallas_call(kern, in_specs=[vmem, vmem, anym, anym, anym], out_specs=[...  58 us
    pallas_call x1, Pallas kernels, m2l(): pl.pallas_call(kern, in_specs=[smem, smem, vmem, vmem, vmem], out_specs=v...  36.5 us
    unnamed x10, local copies, waits for them, and re-layouts  4.67 us
    dot_general x1, local copies, waits for them, and re-layouts, body(): jnp.einsum('bp,cpq->bcq', parent_rounded, l2l_ops, preferred_element_type...  4.44 us
    dot_general x1, matrix products, body(): jnp.einsum('bcp,cpq->bq', leaves, m2m_ops, preferred_element_type=jnp.flo...  2.4 us

profile of v4, /device:TPU:1, one launch (start us, length us, event | category | flops | bytes accessed | tf_op | source)
XLA Modules:
  0.0 112.0 jit_solution(4922426416797593626)
XLA Ops:
  0.0 0.0 copy-start
  0.0 0.2 stack.284
  0.3 0.9 lt.63
  1.1 0.1 lt.64
  1.2 0.8 fusion.13
  2.1 0.1 add_bitcast_fusion
  2.1 0.7 gather_fusion
  2.8 0.9 squeeze.4
  3.8 0.1 copy.15
  3.9 0.1 fusion.11
  4.0 0.1 copy.24
  4.1 0.9 squeeze.5
  5.1 0.1 compare_select_fusion.1
  5.2 0.0 copy-done.3
  5.2 2.4 %fusion.5 = bf16[512,256]{0,1:T(8,128)(2,1)S(1)} fusion(bf16[8,256,256]{2,1,0:T(8,128)(2,1)S(1)} %copy-done.3, bf16[512,8,256]{2,1,0:T(8,128)(2,1)} %bitcast.102), kind=kOutput, calls=%fused_computation.5 | convolution fusion | flops 537001984 | bytes 3407872 | tf_op jit(solution)/shard_map/bcp,cpq->bq/dot_general | solution.py:347
  7.6 0.2 copy.23.refs_1_
  7.8 0.0 copy-start.1
  7.8 4.6 %copy-done.1 = bf16[96,256,256]{2,1,0:T(8,128)(2,1)S(1)} copy-done((bf16[96,256,256]{2,1,0:T(8,128)(2,1)S(1)}, bf16[96,256,256]{2,1,0:T(8,128)(2,1)}, u32[]{:S(2)}) %copy-start.1) | copy-done | bytes 12582936
  12.4 58.0 %exchange.1 = (bf16[16896,2,128]{2,1,0:T(2,128)(2,1)S(1)}, bf16[24576,256]{1,0:T(8,128)(2,1)S(1)}, s32[65536]{0:T(1024)S(1)}, s32[392,128]{1,0:T(8,128)S(1)}) custom-call(s32[21504]{0:T(1024)S(1)} %bitcast.95, bf16[512,2,128]{2,1,0:T(2,128)(2,1)S(1)} %copy.23.refs_1_, bf16[24576,256]{1,0:T(8,128)(2,1)S(1)} %bitcast.93, s32[65536]{0:T(1024)S(1)} %bitcast.94, ...), custom_call_target="tpu_custom_call" | custom-call | tf_op jit(solution)/shard_map/exchange/pallas_call | solution.py:203
  70.4 0.0 copy-done.2
  70.4 36.5 %m2l.1 = bf16[512,256]{1,0:T(8,128)(2,1)S(1)} custom-call(s32[65536]{0:T(1024)S(1)} %get-tuple-element.9.refs_0_, s32[96]{0:T(128)S(1)} %bitcast.97, s32[392,128]{1,0:T(8,128)S(1)} %get-tuple-element.10.refs_2_, bf16[16896,2,128]{2,1,0:T(2,128)(2,1)S(1)} %get-tuple-element.11.refs_3_, bf16[24576,256]{1,0:T(8,128)(2,1)S(1)} %get-tuple-element.12.refs_4_), custom_call_target="tpu_custom_call" | custom-call | tf_op jit(solution)/shard_map/m2l/pallas_call | solution.py:318
  106.9 0.0 copy-done
  106.9 0.7 fusion.8
  107.6 4.4 %copy.32 = f32[512,8,256]{2,1,0:T(8,128)} copy(f32[512,8,256]{2,0,1:T(8,128)S(1)} %fusion.8) | data formatting | bytes 8388608 | tf_op jit(solution)/shard_map/bp,cpq->bcq/dot_general | solution.py:369
  (8 shorter events, 0.1 us)
Async XLA Ops:
  0.0 106.9 %copy-start = (bf16[8,256,256]{2,1,0:T(8,128)(2,1)S(1)}, bf16[8,256,256]{2,1,0:T(8,128)(2,1)}, u32[]{:S(2)}) copy-start(bf16[8,256,256]{2,1,0:T(8,128)(2,1)} %param.11) | copy-start | bytes 3145732
  0.0 5.2 %copy-start.3 = (bf16[8,256,256]{2,1,0:T(8,128)(2,1)S(1)}, bf16[8,256,256]{2,1,0:T(8,128)(2,1)}, u32[]{:S(2)}) copy-start(bf16[8,256,256]{2,1,0:T(8,128)(2,1)} %param.9) | copy-start | bytes 3145732
  7.8 4.6 %copy-start.1 = (bf16[96,256,256]{2,1,0:T(8,128)(2,1)S(1)}, bf16[96,256,256]{2,1,0:T(8,128)(2,1)}, u32[]{:S(2)}) copy-start(bf16[96,256,256]{2,1,0:T(8,128)(2,1)} %param.10) | copy-start | bytes 37748740
  12.4 58.0 %copy-start.2 = (s32[1,96]{1,0:T(1,128)S(1)}, s32[1,96]{1,0:T(1,128)}, u32[]{:S(2)}) copy-start(s32[1,96]{1,0:T(1,128)} %param.15) | copy-start | bytes 1156

commit v5 on v4

--- a/solution.py
+++ b/solution.py
@@ -105,41 +105,40 @@
     def idx_copy(o):
         start, n = groups[o]
         part = pl.ds(start * pair, n * pair)
-        k = slot[o] - 1
-        return remote(idx_in.at[part], land.at[part], idx_send.at[k], idx_recv.at[k], mesh_id(o))
-
-    def idx_local(o):
-        start, n = groups[o]
-        part = pl.ds(start * pair, n * pair)
-        src = idx_in if o == 0 else land
-        return pltpu.make_async_copy(src.at[part], idx.at[part], idx_load.at[slot[o]])
-
+        return remote(idx_in.at[part], land.at[part], idx_send, idx_recv, mesh_id(o))
+
+    mine = pl.ds(0, groups[0][1] * pair)
+    rest = pl.ds(groups[0][1] * pair, (len(order) - groups[0][1]) * pair)
+    load_mine = pltpu.make_async_copy(idx_in.at[mine], idx.at[mine], idx_load.at[0])
+    load_rest = pltpu.make_async_copy(land.at[rest], idx.at[rest], idx_load.at[1])
+    load_mine.start()
+    for c in INTERNAL[1:]:
+        idx_copy(c).start()
     kept = [(own_block, table.at[pl.ds(0, boxes)]), (ops_in, ops_out), (src_in, src_out),
             (tgt_in, tgt_out)]
     kept = [pltpu.make_async_copy(a, b, keep.at[i]) for i, (a, b) in enumerate(kept)]
     for copy in kept:
         copy.start()
+    here = (1 - me_u, me_v)
     children = {o: [c for c in INTERNAL if PARENT[c] == o] for o in INTERNAL}
     loaded = set()
     for kind, o, arg in PLAN:
         if kind == 0:
-            if o == 0:
-                if arg == 0:
-                    idx_local(0).start()
-            else:
+            if o != 0:
+                if 0 in loaded and 1 not in loaded:
+                    remote(idx_in.at[rest], land.at[rest], idx_send, idx_recv, here).wait_recv()
+                    load_rest.start()
+                    loaded.add(1)
                 full_copy(o, arg).wait_recv()
             for c in children[o]:
                 full_copy(c, arg).start()
-            if o == 0 and arg == 1:
-                for c in INTERNAL[1:]:
-                    idx_copy(c).start()
-            if o != 0 and arg == 1:
-                idx_copy(o).wait_recv()
-                idx_local(o).start()
             continue
-        if o not in loaded:
-            idx_local(o).wait()
-            loaded.add(o)
+        if o == 0 and 0 not in loaded:
+            load_mine.wait()
+            loaded.add(0)
+        if o != 0 and 2 not in loaded:
+            load_rest.wait()
+            loaded.add(2)
         block = blocks[o]
         p = pos[arg]
 
@@ -160,7 +159,6 @@
         remote(stage_other.at[p], ghost(1, owner), other_send, other_recv,
                mesh_id(step, 1)).start()
 
-    here = (1 - me_u, me_v)
     inner = len(INTERNAL)
     part = ghost(0, 0, peers - inner)
     side = ghost(1, 0, peers)
@@ -172,8 +170,8 @@
     pltpu.make_async_copy(part, part, own_local).wait()
     for copy in kept:
         copy.wait()
+    remote(idx_in.at[rest], land.at[rest], idx_send, idx_recv, here).wait_send()
     for c in INTERNAL[1:]:
-        idx_copy(c).wait_send()
         for half in range(2):
             full_copy(c, half).wait_send()
 
@@ -218,9 +216,9 @@
             pltpu.VMEM((len(order), cap, 2, coeffs // 2), parents.dtype),
             dma((2 * inner - 2,)),
             dma((2 * inner - 2,)),
-            dma((inner - 1,)),
-            dma((inner - 1,)),
-            dma((inner,)),
+            dma,
+            dma,
+            dma((2,)),
             dma, dma, dma, dma, dma,
             dma((4,)),
         ],
@@ -228,23 +226,30 @@
             collective_id=0, has_side_effects=True, vmem_limit_bytes=20 << 20
         ),
         name="exchange",
-    )(idx, parents.reshape(boxes, 2, coeffs // 2), ops, src, tgt)
+    )(idx, parents.reshape(boxes, 2, coeffs // 2),
+      *(pltpu.with_memory_space_constraint(a, pltpu.HBM) for a in (ops, src, tgt)))
 
 
 def m2l_kernel(ops, chunks_per_op, src_ref, count_ref, tgt_ref, tab_ref, op_ref, out_ref,
                x_ref, y_ref, acc_ref, list_ref):
     boxes, coeffs = acc_ref.shape
-    stride = src_ref.shape[0] // CHUNK
-    empty = ops * chunks_per_op
+    size = src_ref.shape[0]
+    empty = size
     acc_ref[...] = jnp.zeros_like(acc_ref)
     y_ref[...] = jnp.zeros_like(y_ref)
 
     def fill(o, pos):
         n = lax.div(count_ref[o] + (CHUNK - 1), CHUNK)
+        first = lax.div(o, 8) * (8 * CHUNK * chunks_per_op) + lax.rem(o, 8) * CHUNK
         for c in range(chunks_per_op):
-            list_ref[pos] = o * chunks_per_op + c
+            list_ref[pos] = first + c * (8 * CHUNK)
             pos = pos + jnp.where(c < n, 1, 0)
         return pos
+
+    def locate(first):
+        o = lax.div(first, 8 * CHUNK * chunks_per_op) * 8 + lax.rem(lax.div(first, CHUNK), 8)
+        c = lax.rem(lax.div(first, 8 * CHUNK), chunks_per_op)
+        return jnp.minimum(o, ops - 1), c
 
     for i in range(BATCH):
         list_ref[i] = empty
@@ -254,19 +259,19 @@
 
     def gather(it):
         for h in range(BATCH):
-            ch = list_ref[BATCH * it + h]
+            first = list_ref[BATCH * it + h]
+            first = jnp.where(first < empty, first, 0)
             for i in range(CHUNK):
-                s = src_ref.at[pl.ds(i * stride, stride)][ch]
+                s = src_ref.at[pl.ds(i, size - CHUNK + 1)][first]
                 x_ref[h * CHUNK + i] = tab_ref[s].astype(jnp.float32)
 
     def translate(it):
         x2 = x_ref.reshape(2 * BATCH * CHUNK, x_ref.shape[2])
         for h in range(BATCH):
-            ch = list_ref[BATCH * it + h]
+            o, _ = locate(list_ref[BATCH * it + h])
             first = 2 * CHUNK * h
             lo = x2[pl.ds(first, CHUNK, stride=2), :].astype(jnp.bfloat16)
             hi = x2[pl.ds(first + 1, CHUNK, stride=2), :].astype(jnp.bfloat16)
-            o = jnp.minimum(lax.div(ch, chunks_per_op), ops - 1)
             w = op_ref[pl.ds(pl.multiple_of(o * coeffs, coeffs), coeffs), :]
             y_ref[h * CHUNK : (h + 1) * CHUNK, :] = jnp.dot(
                 jnp.concatenate([lo, hi], axis=1), w, preferred_element_type=jnp.float32
@@ -276,7 +281,12 @@
         rows = lax.broadcasted_iota(jnp.int32, (boxes, CHUNK), 0)
         ps = []
         for h in range(BATCH):
-            t = tgt_ref[pl.ds(list_ref[BATCH * it + h], 1), :]
+            first = list_ref[BATCH * it + h]
+            o, c = locate(first)
+            used = jnp.where(first < empty, count_ref[o] - c * CHUNK, 0)
+            first = jnp.where(first < empty, first, 0)
+            t = tgt_ref[pl.ds(lax.div(first, CHUNK), 1), :]
+            t = jnp.where(lax.broadcasted_iota(jnp.int32, (1, CHUNK), 1) < used, t, -1)
             ps.append(jnp.where(rows == t, 1.0, 0.0).astype(jnp.bfloat16))
         acc_ref[...] += jnp.dot(
             jnp.concatenate(ps, axis=1), y_ref[...], preferred_element_type=jnp.float32
@@ -291,17 +301,6 @@
         gather(j + 1)
 
     out_ref[...] = acc_ref[...].astype(out_ref.dtype)
-
-
-def prepare(src, tgt, counts):
-    ops, slots = src.shape
-    chunks = ops * slots // CHUNK
-    position = jnp.arange(slots, dtype=jnp.int32)[None, :]
-    tgt = jnp.where(position < counts[:, None], tgt, -1)
-    tgt = jnp.pad(tgt.reshape(-1, CHUNK), ((0, 8), (0, 0)), constant_values=-1)
-    stride = -(-(chunks + 1) // 128) * 128
-    src = jnp.pad(src.reshape(-1, CHUNK).T, ((0, 0), (0, stride - chunks))).reshape(-1)
-    return src, tgt
 
 
 def m2l(table, src, tgt, counts, m2l_ops, slots, boxes):
@@ -361,10 +360,14 @@
     )
     src = jnp.where(sources < box_count, sources, shifted)
     src = jnp.clip(src, 0, rows - 1)
-    src, tgt = prepare(src, task_target[0], task_count[0])
+    slots = src.shape[1]
+    src, tgt = (
+        a.reshape(-1, 8, slots // CHUNK, CHUNK).transpose(0, 2, 1, 3).reshape(-1, CHUNK)
+        for a in (src, task_target[0])
+    )
+    src = src.reshape(-1)
     ops = m2l_ops.reshape(-1, coeff_count)
     table, ops, src, tgt = exchange(parents, lists, ops, src, tgt)
-    slots = task_target.shape[2]
     parent_rounded = m2l(table, src, tgt, task_count[0], ops, slots, box_count)
     leaf_local = jnp.einsum(
         "bp,cpq->bcq", parent_rounded, l2l_ops, preferred_element_type=jnp.float32

time: 112 us -> 104 us (0.929)
  local copies, waits for them, and re-layouts: 13.2 us -> 5.52 us
  Pallas kernels: 94.5 us -> 91.9 us
  other arithmetic: 1.1 us -> 2.64 us
    unnamed x10 -> x4, local copies, waits for them, and re-layouts: 4.67 us -> 0.01 us
    squeeze x3 -> x0, local copies, waits for them, and re-layouts: 2.01 us -> none  [the longest x2 1.07 us: body(): sources = task_source[0]]
    pallas_call x1, Pallas kernels: 58 us -> 56.1 us  [exchange(): pl.pallas_call(kern, in_specs=[vmem, vmem, anym, anym, anym], out_specs=[...]
    min x0 -> x1, other arithmetic: none -> 1.71 us  [body(): src = jnp.clip(src, 0, rows - 1)]
where the time goes in v5:
time: 104 us
  Pallas kernels  91.9 us (88%)
  local copies, waits for them, and re-layouts  5.52 us (5%)
  matrix products  3.38 us (3%)
  other arithmetic  2.64 us (3%)
    pallas_call x1, Pallas kernels, exchange(): pl.pallas_call(kern, in_specs=[vmem, vmem, anym, anym, anym], out_specs=[...  56.1 us
    pallas_call x1, Pallas kernels, m2l(): pl.pallas_call(kern, in_specs=[smem, smem, vmem, vmem, vmem], out_specs=v...  35.9 us
    dot_general x1, local copies, waits for them, and re-layouts, body(): jnp.einsum('bp,cpq->bcq', parent_rounded, l2l_ops, preferred_element_type...  4.44 us
    dot_general x1, matrix products, body(): jnp.einsum('bcp,cpq->bq', leaves, m2m_ops, preferred_element_type=jnp.flo...  2.66 us

profile of v5, /device:TPU:1, one launch (start us, length us, event | category | flops | bytes accessed | tf_op | source)
XLA Modules:
  0.0 103.6 jit_solution(10669378611325880328)
XLA Ops:
  0.0 0.0 copy-start
  0.0 0.2 stack.284
  0.2 0.9 fusion.15
  1.1 0.1 add_bitcast_fusion
  1.2 0.7 gather_fusion
  1.9 1.7 %fusion.10 = s32[12,8,4,128]{3,1,2,0:T(8,128)} fusion(s32[1,96,512]{2,1,0:T(8,128)} %param.13, pred[]{:T(512)S(6)} %eq.7), kind=kLoop, calls=%fused_computation.9 | loop fusion | flops 491520 | bytes 393217 | tf_op jit(solution)/shard_map/jit(clip)/min | solution.py:362
  3.6 2.7 %fusion.5 = bf16[512,256]{0,1:T(8,128)(2,1)S(1)} fusion(bf16[8,256,256]{2,1,0:T(8,128)(2,1)} %param.9, bf16[512,8,256]{2,1,0:T(8,128)(2,1)} %bitcast.123), kind=kOutput, calls=%fused_computation.5 | convolution fusion | flops 537001984 | bytes 3407872 | tf_op jit(solution)/shard_map/bcp,cpq->bq/dot_general | solution.py:346
  6.2 0.2 copy.17.refs_1_
  6.4 0.0 copy-start.1
  6.4 56.1 %exchange.1 = (bf16[16896,2,128]{2,1,0:T(2,128)(2,1)S(1)}, bf16[24576,256]{1,0:T(8,128)(2,1)S(1)}, s32[49152]{0:T(1024)S(1)}, s32[384,128]{1,0:T(8,128)S(1)}) custom-call(s32[21504]{0:T(1024)S(1)} %bitcast.115, bf16[512,2,128]{2,1,0:T(2,128)(2,1)S(1)} %copy.17.refs_1_, bf16[24576,256]{1,0:T(8,128)(2,1)} %bitcast.117, s32[49152]{0:T(1024)} %bitcast.118, ...), custom_call_target="tpu_custom_call" | custom-call | tf_op jit(solution)/shard_map/exchange/pallas_call | solution.py:201
  62.5 0.0 copy-done.1
  62.5 35.9 %m2l.1 = bf16[512,256]{1,0:T(8,128)(2,1)S(1)} custom-call(s32[49152]{0:T(1024)S(1)} %get-tuple-element.9.refs_0_, s32[96]{0:T(128)S(1)} %bitcast.116, s32[384,128]{1,0:T(8,128)S(1)} %get-tuple-element.10.refs_2_, bf16[16896,2,128]{2,1,0:T(2,128)(2,1)S(1)} %get-tuple-element.11.refs_3_, bf16[24576,256]{1,0:T(8,128)(2,1)S(1)} %get-tuple-element.12.refs_4_), custom_call_target="tpu_custom_call" | custom-call | tf_op jit(solution)/shard_map/m2l/pallas_call | solution.py:317
  98.4 0.0 copy-done
  98.4 0.7 fusion.8
  99.1 4.4 %copy.25 = f32[512,8,256]{2,1,0:T(8,128)} copy(f32[512,8,256]{2,0,1:T(8,128)S(1)} %fusion.8) | data formatting | bytes 8388608 | tf_op jit(solution)/shard_map/bp,cpq->bcq/dot_general | solution.py:372
  (2 shorter events, 0.0 us)
Async XLA Ops:
  0.0 98.4 %copy-start = (bf16[8,256,256]{2,1,0:T(8,128)(2,1)S(1)}, bf16[8,256,256]{2,1,0:T(8,128)(2,1)}, u32[]{:S(2)}) copy-start(bf16[8,256,256]{2,1,0:T(8,128)(2,1)} %param.11) | copy-start | bytes 3145732
  6.4 56.1 %copy-start.1 = (s32[1,96]{1,0:T(1,128)S(1)}, s32[1,96]{1,0:T(1,128)}, u32[]{:S(2)}) copy-start(s32[1,96]{1,0:T(1,128)} %param.15) | copy-start | bytes 1156

commit v6 on v5

--- a/solution.py
+++ b/solution.py
@@ -57,7 +57,8 @@
     return parts[0] + parts[1] + parts[2]
 
 
-def comm_kernel(peers, idx_in, own_block, ops_in, src_in, tgt_in, table, ops_out, src_out, tgt_out, *scratch):
+def comm_kernel(peers, idx_in, own_block, ops_in, src_in, tgt_in, l2l_in, table,
+                ops_out, src_out, tgt_out, l2l_out, *scratch):
     blocks = dict(zip(INTERNAL, (own_block,) + scratch[: len(INTERNAL) - 1]))
     scratch = scratch[len(INTERNAL) - 1 :]
     (land, idx, stage_own, stage_other, full_send, full_recv, idx_send, idx_recv, idx_load,
@@ -115,7 +116,7 @@
     for c in INTERNAL[1:]:
         idx_copy(c).start()
     kept = [(own_block, table.at[pl.ds(0, boxes)]), (ops_in, ops_out), (src_in, src_out),
-            (tgt_in, tgt_out)]
+            (tgt_in, tgt_out), (l2l_in, l2l_out)]
     kept = [pltpu.make_async_copy(a, b, keep.at[i]) for i, (a, b) in enumerate(kept)]
     for copy in kept:
         copy.start()
@@ -170,6 +171,12 @@
     pltpu.make_async_copy(part, part, own_local).wait()
     for copy in kept:
         copy.wait()
+    block = peers * cap
+    rows = src_out[...]
+    first = jnp.logical_and(rows >= boxes, rows < boxes + block)
+    moved = jnp.where(jnp.logical_and(me_u == 1, first), rows + block, rows - block)
+    rows = jnp.where(rows < boxes, rows, moved)
+    src_out[...] = jnp.clip(rows, 0, boxes + 2 * block - 1)
     remote(idx_in.at[rest], land.at[rest], idx_send, idx_recv, here).wait_send()
     for c in INTERNAL[1:]:
         for half in range(2):
@@ -183,7 +190,7 @@
     return step
 
 
-def exchange(parents, lists, ops, src, tgt):
+def exchange(parents, lists, ops, src, tgt, l2l):
     _, peers, cap = lists.shape
     boxes, coeffs = parents.shape
     groups, order, pos = list_layout()
@@ -200,13 +207,14 @@
 
     return pl.pallas_call(
         kern,
-        in_specs=[vmem, vmem, anym, anym, anym],
-        out_specs=[vmem] * 4,
+        in_specs=[vmem, vmem, anym, anym, anym, anym],
+        out_specs=[vmem] * 5,
         out_shape=[
             pltpu.VMEM((boxes + 2 * peers * cap, 2, coeffs // 2), parents.dtype),
             pltpu.VMEM(ops.shape, ops.dtype),
             pltpu.VMEM(src.shape, src.dtype),
             pltpu.VMEM(tgt.shape, tgt.dtype),
+            pltpu.VMEM(l2l.shape, l2l.dtype),
         ],
         scratch_shapes=[pltpu.VMEM((boxes, 2, coeffs // 2), parents.dtype)] * (inner - 1)
         + [
@@ -220,18 +228,18 @@
             dma,
             dma((2,)),
             dma, dma, dma, dma, dma,
-            dma((4,)),
+            dma((5,)),
         ],
         compiler_params=pltpu.CompilerParams(
             collective_id=0, has_side_effects=True, vmem_limit_bytes=20 << 20
         ),
         name="exchange",
     )(idx, parents.reshape(boxes, 2, coeffs // 2),
-      *(pltpu.with_memory_space_constraint(a, pltpu.HBM) for a in (ops, src, tgt)))
-
-
-def m2l_kernel(ops, chunks_per_op, src_ref, count_ref, tgt_ref, tab_ref, op_ref, out_ref,
-               x_ref, y_ref, acc_ref, list_ref):
+      *(pltpu.with_memory_space_constraint(a, pltpu.HBM) for a in (ops, src, tgt, l2l)))
+
+
+def m2l_kernel(ops, chunks_per_op, src_ref, count_ref, tgt_ref, tab_ref, op_ref, l2l_ref, out_hbm,
+               x_ref, y_ref, acc_ref, list_ref, leaf_ref, sem):
     boxes, coeffs = acc_ref.shape
     size = src_ref.shape[0]
     empty = size
@@ -300,14 +308,34 @@
         translate(j)
         gather(j + 1)
 
-    out_ref[...] = acc_ref[...].astype(out_ref.dtype)
-
-
-def m2l(table, src, tgt, counts, m2l_ops, slots, boxes):
+    half = boxes // 2
+    octants = l2l_ref.shape[0] // coeffs
+    span = half * octants
+    lanes = leaf_ref.shape[2]
+    sends = []
+    for k in range(2):
+        parent = acc_ref[k * half : (k + 1) * half, :].astype(jnp.bfloat16)
+        for c in range(octants):
+            leaf = jnp.dot(parent, l2l_ref[c * coeffs : (c + 1) * coeffs, :],
+                           preferred_element_type=jnp.float32)
+            for p in range(2):
+                leaf_ref[p, pl.ds(k * span + c, half, stride=octants), :] = (
+                    leaf[:, p * lanes : (p + 1) * lanes])
+        for p in range(2):
+            sends.append(pltpu.make_async_copy(
+                leaf_ref.at[p, pl.ds(k * span, span)],
+                out_hbm.at[pl.ds(k * span, span), pl.ds(p * lanes, lanes)], sem.at[2 * k + p]))
+            sends[-1].start()
+    for send in sends:
+        send.wait()
+
+
+def m2l(table, src, tgt, counts, m2l_ops, l2l, slots, boxes):
     ops = counts.shape[0]
     coeffs = m2l_ops.shape[1]
     chunks_per_op = slots // CHUNK
     chunks = ops * chunks_per_op
+    octants = l2l.shape[0] // coeffs
     smem = pl.BlockSpec(memory_space=pltpu.SMEM)
     vmem = pl.BlockSpec(memory_space=pltpu.VMEM)
 
@@ -316,14 +344,16 @@
 
     return pl.pallas_call(
         kern,
-        in_specs=[smem, smem, vmem, vmem, vmem],
-        out_specs=vmem,
-        out_shape=jax.ShapeDtypeStruct((boxes, coeffs), jnp.bfloat16),
+        in_specs=[smem, smem, vmem, vmem, vmem, vmem],
+        out_specs=pl.BlockSpec(memory_space=pl.ANY),
+        out_shape=jax.ShapeDtypeStruct((boxes * octants, coeffs), jnp.float32),
         scratch_shapes=[
             pltpu.VMEM((BATCH * CHUNK, 2, coeffs // 2), jnp.float32),
             pltpu.VMEM((BATCH * CHUNK, coeffs), jnp.bfloat16),
             pltpu.VMEM((boxes, coeffs), jnp.float32),
             pltpu.SMEM((chunks + 4 * BATCH,), jnp.int32),
+            pltpu.VMEM((2, boxes * octants, coeffs // 2), jnp.float32),
+            pltpu.SemaphoreType.DMA((4,)),
         ],
         compiler_params=pltpu.CompilerParams(vmem_limit_bytes=8 << 20),
         name="m2l",
@@ -333,6 +363,7 @@
         pltpu.with_memory_space_constraint(tgt, pltpu.VMEM),
         pltpu.with_memory_space_constraint(table, pltpu.VMEM),
         pltpu.with_memory_space_constraint(m2l_ops, pltpu.VMEM),
+        pltpu.with_memory_space_constraint(l2l, pltpu.VMEM),
     )
 
 
@@ -351,28 +382,15 @@
     peers = boxes.shape[1]
     other = jnp.where(column == 0, boxes[2], boxes[0])
     lists = jnp.stack([boxes[1], other], 0)
-    sources = task_source[0]
-    block = peers * cap
-    rows = box_count + 2 * block
-    own = jnp.logical_and(sources >= box_count, sources < box_count + block)
-    shifted = jnp.where(
-        jnp.logical_and(column == 1, own), sources + block, sources - block
+    slots = task_source.shape[2]
+    src, tgt = (
+        a[0].reshape(-1, 8, slots // CHUNK, CHUNK).transpose(0, 2, 1, 3).reshape(-1, CHUNK)
+        for a in (task_source, task_target)
     )
-    src = jnp.where(sources < box_count, sources, shifted)
-    src = jnp.clip(src, 0, rows - 1)
-    slots = src.shape[1]
-    src, tgt = (
-        a.reshape(-1, 8, slots // CHUNK, CHUNK).transpose(0, 2, 1, 3).reshape(-1, CHUNK)
-        for a in (src, task_target[0])
-    )
-    src = src.reshape(-1)
     ops = m2l_ops.reshape(-1, coeff_count)
-    table, ops, src, tgt = exchange(parents, lists, ops, src, tgt)
-    parent_rounded = m2l(table, src, tgt, task_count[0], ops, slots, box_count)
-    leaf_local = jnp.einsum(
-        "bp,cpq->bcq", parent_rounded, l2l_ops, preferred_element_type=jnp.float32
-    )
-    return leaf_local.reshape(-1, coeff_count)
+    l2l = l2l_ops.reshape(-1, coeff_count)
+    table, ops, src, tgt, l2l = exchange(parents, lists, ops, src, tgt, l2l)
+    return m2l(table, src.reshape(-1), tgt, task_count[0], ops, l2l, slots, box_count)
 
 
 def solution(mesh):

time: 104 us -> 98.6 us (0.948)
  the two profiles are of different devices: /device:TPU:1 before, /device:TPU:35 now
where the time goes in v6:
time: 98.6 us; the launch traced here: 96.8 us
  Pallas kernels  92.4 us (94%)
  matrix products  2.4 us (2%)
  local copies, waits for them, and re-layouts  1.07 us (1%)
    pallas_call x1, Pallas kernels, exchange(): pl.pallas_call(kern, in_specs=[vmem, vmem, anym, anym, anym, anym], out_s...  53.5 us
    pallas_call x1, Pallas kernels, m2l(): pl.pallas_call(kern, in_specs=[smem, smem, vmem, vmem, vmem, vmem], out_s...  38.9 us
    dot_general x1, matrix products, body(): jnp.einsum('bcp,cpq->bq', leaves, m2m_ops, preferred_element_type=jnp.flo...  2.4 us

profile of v6, /device:TPU:35, one launch (start us, length us, event | category | flops | bytes accessed | tf_op | source)
XLA Modules:
  0.0 96.8 jit_solution(8568929230824514637)
XLA Ops:
  0.0 0.0 copy-start
  0.0 0.2 stack.284
  0.2 0.9 fusion.9
  1.1 0.1 add_bitcast_fusion
  1.2 0.7 gather_fusion
  1.9 0.0 copy-done
  1.9 2.4 %fusion.5 = bf16[512,256]{0,1:T(8,128)(2,1)S(1)} fusion(bf16[8,256,256]{2,1,0:T(8,128)(2,1)S(1)} %copy-done, bf16[512,8,256]{2,1,0:T(8,128)(2,1)} %bitcast.102), kind=kOutput, calls=%fused_computation.4 | convolution fusion | flops 537001984 | bytes 3407872 | tf_op jit(solution)/shard_map/bcp,cpq->bq/dot_general | solution.py:377
  4.3 0.2 copy.16.refs_1_
  4.4 0.0 copy-start.1
  4.5 53.5 %exchange.1 = (bf16[16896,2,128]{2,1,0:T(2,128)(2,1)S(1)}, bf16[24576,256]{1,0:T(8,128)(2,1)S(1)}, s32[384,128]{1,0:T(8,128)S(1)}, s32[384,128]{1,0:T(8,128)S(1)}, bf16[2048,256]{1,0:T(8,128)(2,1)S(1)}) custom-call(s32[21504]{0:T(1024)S(1)} %bitcast.92, bf16[512,2,128]{2,1,0:T(2,128)(2,1)S(1)} %copy.16.refs_1_, bf16[24576,256]{1,0:T(8,128)(2,1)} %bitcast.95, ...), custom_call_target="tpu_custom_call" | custom-call | tf_op jit(solution)/shard_map/exchange/pallas_call | solution.py:208
  57.9 0.0 copy-done.1
  57.9 38.9 %m2l.1 = f32[4096,256]{1,0:T(8,128)} custom-call(s32[49152]{0:T(1024)S(1)} %bitcast.93, s32[96]{0:T(128)S(1)} %bitcast.94, s32[384,128]{1,0:T(8,128)S(1)} %get-tuple-element.11.refs_2_, bf16[16896,2,128]{2,1,0:T(2,128)(2,1)S(1)} %get-tuple-element.12.refs_3_, bf16[24576,256]{1,0:T(8,128)(2,1)S(1)} %get-tuple-element.13.refs_4_, ...), custom_call_target="tpu_custom_call" | custom-call | tf_op jit(solution)/shard_map/m2l/pallas_call | solution.py:345
  (2 shorter events, 0.0 us)
Async XLA Ops:
  0.0 1.9 %copy-start = (bf16[8,256,256]{2,1,0:T(8,128)(2,1)S(1)}, bf16[8,256,256]{2,1,0:T(8,128)(2,1)}, u32[]{:S(2)}) copy-start(bf16[8,256,256]{2,1,0:T(8,128)(2,1)} %param.9) | copy-start | bytes 3145732
  4.4 53.5 %copy-start.1 = (s32[1,96]{1,0:T(1,128)S(1)}, s32[1,96]{1,0:T(1,128)}, u32[]{:S(2)}) copy-start(s32[1,96]{1,0:T(1,128)} %param.15) | copy-start | bytes 1156
